TPU v7x, 256 devices: a whole 4x4x8 slice. The times are simulated.
256 devices in a mesh: lat: 16 (over y_lo, x, core), lon: 16 (over z, y_hi).
Axes of the slice: x: 4, y: 4 (y_hi: 2, y_lo: 2; y = y_hi * 2 + y_lo), z: 8, core: 2. Of those that a mesh axis runs over, the one named last changes fastest.
Arguments:
- tokens: bfloat16 [256, 256, 1024], P('lat', 'lon'), may hold values from -36 to 36
- gain_attn: float32 [1024], replicated, may hold values from 0.5 to 1.5
- w_qkv: bfloat16 [1024, 1536], replicated, may hold values from -0.1875 to 0.1875
- logit_scale: float32 [8], replicated, may hold values from 4 to 20
- w_out: bfloat16 [512, 1024], replicated, may hold values from -0.5 to 0.5
- gain_ffn: float32 [1024], replicated, may hold values from 0.5 to 1.5
- w_up: bfloat16 [1024, 2048], replicated, may hold values from -0.1875 to 0.1875
- conv_taps: float32 [3, 3, 2048], replicated, may hold values from -2 to 2
Outputs:
- ffn_hidden: bfloat16 [256, 256, 2048], P('lat', 'lon')
All inputs are finite; a program needn't handle non-finite values.
Results may differ from a plain program's by a relative error of at most 0.008.
Values may be sent and summed in bfloat16 or wider, within the bound.
A program may use at most 64 MiB of HBM per device.

v0:
```python
import jax
import jax.numpy as jnp
from jax import lax
from jax.sharding import PartitionSpec as P

D = 1024
HEADS = 8
HEAD_DIM = 64
HID = 2048
RADIUS = 6
INNER = 512


def with_halo(x, sides, width):
    for axis, dim in sides:
        size, length = (lax.axis_size(axis), x.shape[dim])
        up = [(i, (i + 1) % size) for i in range(size)]
        down = [(j, i) for i, j in up]
        last = lax.slice_in_dim(x, length - width, length, axis=dim)
        leading = lax.slice_in_dim(x, 0, width, axis=dim)
        before = lax.ppermute(last, axis, up)
        after = lax.ppermute(leading, axis, down)
        x = jnp.concatenate([before, x, after], axis=dim)
    return x


def layer_norm(values_in, gain):
    widened = values_in.astype(jnp.float32)
    centre = jnp.mean(widened, -1, keepdims=True)
    spread = jnp.mean((widened - centre) ** 2, -1, keepdims=True)
    return (widened - centre) * lax.rsqrt(spread + 1e-05) * gain


def heads_norm(vectors, factor):
    return vectors * lax.rsqrt(jnp.sum(vectors * vectors, -1, keepdims=True) + 1e-06) * factor


def lat_inside(first, count, lat_total):
    position = first + jnp.arange(count, dtype=jnp.int32)
    return (position >= 0) & (position < lat_total)


def strip_attend(query_block, key_block, value_block, allowed):
    results = []
    for head in range(HEADS):
        lower = head * HEAD_DIM
        scores = lax.dot_general(
            query_block[:, lower : lower + HEAD_DIM],
            key_block[:, lower : lower + HEAD_DIM],
            (((1,), (1,)), ((), ())),
            preferred_element_type=jnp.float32,
        )
        weights = jnp.where(allowed, jnp.exp(scores), 0.0)
        denominator = jnp.sum(weights, -1, keepdims=True)
        summed = jnp.dot(
            weights.astype(jnp.bfloat16),
            value_block[:, lower : lower + HEAD_DIM],
            preferred_element_type=jnp.float32,
        )
        results.append(summed / denominator)
    return jnp.concatenate(results, -1).astype(jnp.bfloat16)


def attend(queries, key_grid, value_grid, q_rows, q_cols, k_rows, k_cols, key_rows_ok):
    strip = 1
    for candidate in range(1, q_rows + 1):
        if q_rows % candidate == 0 and candidate * q_cols <= 512:
            strip = candidate
    key_strip = strip + 2 * RADIUS
    margin = (k_rows - q_rows) // 2
    row_gap = jnp.arange(key_strip)[None, :] - jnp.arange(strip)[:, None] - margin
    col_gap = jnp.arange(k_cols)[None, :] - jnp.arange(q_cols)[:, None] - margin
    col_ok = jnp.abs(col_gap) <= RADIUS
    key_block = key_grid.reshape(key_strip * k_cols, INNER)
    value_block = value_grid.reshape(key_strip * k_cols, INNER)
    row_ok = (jnp.abs(row_gap) <= RADIUS) & key_rows_ok[None, :]
    allowed = (row_ok[:, None, :, None] & col_ok[None, :, None, :]).reshape(
        strip * q_cols, key_strip * k_cols
    )
    outputs = strip_attend(queries, key_block, value_block, allowed)
    return outputs


def on_device(tokens, gain_attn, w_qkv, logit_scale, w_out, gain_ffn, w_up, conv_taps):
    height, breadth = (tokens.shape[0], tokens.shape[1])
    lat_total = height * lax.axis_size("lat")
    lat_first = lax.axis_index("lat") * height
    normed = layer_norm(tokens, gain_attn).astype(jnp.bfloat16).reshape(height * breadth, D)
    projected = jnp.dot(normed, w_qkv, preferred_element_type=jnp.float32)
    queries = (
        heads_norm(projected[:, :INNER].reshape(-1, HEADS, HEAD_DIM), logit_scale[:, None])
        .astype(jnp.bfloat16)
        .reshape(height * breadth, INNER)
    )
    key_heads = heads_norm(
        projected[:, INNER : 2 * INNER].reshape(-1, HEADS, HEAD_DIM), 1.0
    ).astype(jnp.bfloat16)
    values = projected[:, 2 * INNER :].astype(jnp.bfloat16)
    packed = jnp.concatenate(
        [key_heads.reshape(height, breadth, INNER), values.reshape(height, breadth, INNER)], -1
    )
    widened = with_halo(packed, (("lat", 0), ("lon", 1)), RADIUS)
    k_rows, k_cols = (height + 2 * RADIUS, breadth + 2 * RADIUS)
    key_rows_ok = lat_inside(lat_first - RADIUS, k_rows, lat_total)
    attended = attend(
        queries,
        widened[:, :, :INNER],
        widened[:, :, INNER:],
        height,
        breadth,
        k_rows,
        k_cols,
        key_rows_ok,
    )
    stream = tokens.astype(jnp.float32).reshape(height * breadth, D) + jnp.dot(
        attended, w_out, preferred_element_type=jnp.float32
    )
    normed_ffn = layer_norm(stream, gain_ffn).astype(jnp.bfloat16)
    hidden = (
        jnp.dot(normed_ffn, w_up, preferred_element_type=jnp.float32)
        .astype(jnp.bfloat16)
        .reshape(height, breadth, HID)
    )
    padded = with_halo(hidden, (("lat", 0), ("lon", 1)), 1)
    rows_ok = lat_inside(lat_first - 1, height + 2, lat_total)
    padded = jnp.where(rows_ok[:, None, None], padded, jnp.zeros_like(padded))
    filtered = jnp.zeros((height, breadth, HID), jnp.float32)
    for row_tap in range(3):
        for col_tap in range(3):
            filtered = (
                filtered
                + padded[row_tap : row_tap + height, col_tap : col_tap + breadth].astype(
                    jnp.float32
                )
                * conv_taps[row_tap, col_tap]
            )
    return jax.nn.gelu(filtered, approximate=False).astype(jnp.bfloat16)


def solution(mesh):
    in_specs = (P("lat", "lon", None), P(), P(), P(), P(), P(), P(), P())
    out_specs = P("lat", "lon", None)
    return jax.shard_map(
        on_device, mesh=mesh, in_specs=in_specs, out_specs=out_specs, check_vma=False
    )
```

profile of v0, /device:TPU:0, one launch (start us, length us, event | category | flops | bytes accessed | tf_op | source)
XLA Modules:
  0.0 126.7 jit_solution(335100722193907488)
XLA Ops:
  7.1 2.0 %copy.21 = f32[256,512]{0,1:T(8,128)} copy(f32[256,512]{1,0:T(8,128)} %slice_multiply_fusion) | data formatting | bytes 1048576 | tf_op jit(solution)/shard_map/mul | solution.py:35
  11.1 2.0 %copy.22 = f32[256,512]{1,0:T(8,128)} copy(f32[256,512]{0,1:T(8,128)} %bitcast.43) | data formatting | bytes 1048576 | tf_op jit(solution)/shard_map/mul | solution.py:35
  13.2 2.5 %multiply_convert_fusion.4 = (bf16[256,512]{1,0:T(8,128)(2,1)}, f32[256,512]{1,0:T(8,128)}, f32[256,512]{1,0:T(8,128)}) fusion(f32[256,512]{1,0:T(8,128)} %copy.22, f32[256,1536]{1,0:T(8,128)} %copy-done.2, f32[512]{0:T(512)S(1)} %mul.198), kind=kLoop, calls=%fused_computation.78 | loop fusion | flops 524288 | bytes 2885632 | tf_op jit(solution)/shard_map/convert_element_type | solution.py:92
  15.8 2.0 %copy.23 = f32[256,512]{0,1:T(8,128)} copy(f32[256,512]{1,0:T(8,128)} %get-tuple-element.8) | data formatting | bytes 1048576 | tf_op jit(solution)/shard_map/mul | solution.py:35
  20.4 2.3 %mul.204 = f32[16,16,512]{2,1,0:T(8,128)} reshape(f32[256,8,64]{2,1,0:T(8,128)} %mul.203) | data formatting | bytes 1048576 | tf_op jit(solution)/shard_map/mul | solution.py:35
  23.9 1.7 %pad_maximum_fusion.3 = (bf16[6,16,1024]{2,1,0:T(8,128)(2,1)}, bf16[6,16,1024]{2,1,0:T(8,128)(2,1)}) fusion(bf16[16,16,512]{2,1,0:T(8,128)(2,1)} %bitcast.38, bf16[16,16,512]{2,1,0:T(8,128)(2,1)S(1)} %multiply_convert_fusion.3), kind=kLoop, calls=%fused_computation.105 | loop fusion | flops 786432 | bytes 917504 | tf_op jit(solution)/shard_map/slice | solution.py:19
  25.7 1.5 %collective-permute-start.1 = (bf16[6,16,1024]{2,1,0:T(8,128)(2,1)}, bf16[6,16,1024]{2,1,0:T(8,128)(2,1)}, u32[]{:S(2)}, u32[]{:S(2)}) collective-permute-start(bf16[6,16,1024]{2,1,0:T(8,128)(2,1)} %get-tuple-element.17), channel_id=1, source_target_pairs={{16,0},{32,16},{48,32},{64,48},{80,64},{96,80},{112,96},{128,112},... | collective-permute-start | bytes 589832 | tf_op jit(solution)/shard_map/ppermute | solution.py:22
  27.2 3.5 %collective-permute-done.1 = bf16[6,16,1024]{2,1,0:T(8,128)(2,1)} collective-permute-done((bf16[6,16,1024]{2,1,0:T(8,128)(2,1)}, bf16[6,16,1024]{2,1,0:T(8,128)(2,1)}, u32[]{:S(2)}, u32[]{:S(2)}) %collective-permute-start.1) | collective-permute-done | bytes 196640 | tf_op jit(solution)/shard_map/ppermute | solution.py:22
  30.7 4.0 %collective-permute-done = bf16[6,16,1024]{2,1,0:T(8,128)(2,1)} collective-permute-done((bf16[6,16,1024]{2,1,0:T(8,128)(2,1)}, bf16[6,16,1024]{2,1,0:T(8,128)(2,1)}, u32[]{:S(2)}, u32[]{:S(2)}) %collective-permute-start) | collective-permute-done | bytes 196640 | tf_op jit(solution)/shard_map/ppermute | solution.py:21
  37.0 8.2 %collective-permute-start.3 = (bf16[28,6,1024]{2,1,0:T(8,128)(2,1)}, bf16[28,6,1024]{2,1,0:T(8,128)(2,1)}, u32[]{:S(2)}, u32[]{:S(2)}) collective-permute-start(bf16[28,6,1024]{2,1,0:T(8,128)(2,1)} %get-tuple-element.15), channel_id=1, source_target_pairs={{1,0},{2,1},{3,2},{4,3},{5,4},{6,5},{7,6},{8,7},{9,8},{10,9},{11,1... | collective-permute-start | bytes 1032200 | tf_op jit(solution)/shard_map/ppermute | solution.py:22
  45.2 1.5 %broadcast_and_fusion = pred[16,16,28,28]{3,2,1,0:T(8,128)(4,1)} fusion(pred[16,28]{1,0:T(8,128)(4,1)S(1)} %get-tuple-element.45, pred[16,28]{1,0:T(8,128)(4,1)S(1)} %get-tuple-element.46), kind=kLoop, calls=%fused_computation.21 | loop fusion | flops 200704 | bytes 201600 | tf_op jit(solution)/shard_map/and | solution.py:77
  46.7 4.7 %and.51 = pred[256,784]{1,0:T(8,128)(4,1)} reshape(pred[16,16,28,28]{3,2,1,0:T(8,128)(4,1)} %broadcast_and_fusion) | data formatting | bytes 401408 | tf_op jit(solution)/shard_map/and | solution.py:77
  51.4 1.9 %copy.25 = pred[256,784]{0,1:T(8,128)(4,1)} copy(pred[256,784]{1,0:T(8,128)(4,1)} %and.51) | data formatting | bytes 401408 | tf_op jit(solution)/shard_map/and | solution.py:77
  53.3 4.3 %collective-permute-done.2 = bf16[28,6,1024]{2,1,0:T(8,128)(2,1)} collective-permute-done((bf16[28,6,1024]{2,1,0:T(8,128)(2,1)}, bf16[28,6,1024]{2,1,0:T(8,128)(2,1)}, u32[]{:S(2)}, u32[]{:S(2)}) %collective-permute-start.2) | collective-permute-done | bytes 344096 | tf_op jit(solution)/shard_map/ppermute | solution.py:21
  57.6 2.3 %pad_maximum_fusion = bf16[28,28,1024]{2,1,0:T(8,128)(2,1)S(1)} fusion(bf16[28,6,1024]{2,1,0:T(8,128)(2,1)} %collective-permute-done.3, bf16[6,16,1024]{2,1,0:T(8,128)(2,1)} %collective-permute-done.1, bf16[16,16,512]{2,1,0:T(8,128)(2,1)} %bitcast.40, bf16[16,16,512]{2,1,0:T(8,128)(2,1)S(1)} %multiply_convert_fusion.3, ...), kind=kLoop, calls=%fused_computation.22 | loop fusion | flops 9633792 | bytes 3211264 | tf_op jit(solution)/shard_map/concatenate | solution.py:23
  61.3 2.1 %reshape.143 = bf16[784,512]{1,0:T(8,128)(2,1)} reshape(bf16[28,28,512]{2,1,0:T(8,128)(2,1)} %get-tuple-element.6) | data formatting | bytes 1605632 | tf_op jit(solution)/shard_map/reshape | solution.py:74
  63.4 2.8 %fusion.72 = (f32[256]{0:T(256)}, bf16[256,784]{0,1:T(8,128)(2,1)}) fusion(pred[256,784]{0,1:T(8,128)(4,1)} %copy.25, bf16[784,512]{1,0:T(8,128)(2,1)} %reshape.143, bf16[256,512]{1,0:T(8,128)(2,1)S(1)} %copy-done.7), kind=kOutput, calls=%fused_computation.133 | convolution fusion | flops 26291968 | bytes 869376 | tf_op jit(solution)/shard_map/dot_general | solution.py:47
  66.2 2.8 %fusion.73 = (f32[256]{0:T(256)}, bf16[256,784]{0,1:T(8,128)(2,1)}) fusion(pred[256,784]{0,1:T(8,128)(4,1)} %copy.25, bf16[784,512]{1,0:T(8,128)(2,1)} %reshape.143, bf16[256,512]{1,0:T(8,128)(2,1)S(1)} %copy-done.7), kind=kOutput, calls=%fused_computation.134 | convolution fusion | flops 26291968 | bytes 869376 | tf_op jit(solution)/shard_map/dot_general | solution.py:47
  69.0 1.7 %fusion.74 = (f32[256]{0:T(256)}, bf16[256,784]{0,1:T(8,128)(2,1)}) fusion(pred[256,784]{0,1:T(8,128)(4,1)S(1)} %copy-done.8, bf16[784,512]{1,0:T(8,128)(2,1)S(1)} %copy-done.6, bf16[256,512]{1,0:T(8,128)(2,1)S(1)} %copy-done.7), kind=kOutput, calls=%fused_computation.135 | convolution fusion | flops 26291968 | bytes 869376 | tf_op jit(solution)/shard_map/dot_general | solution.py:47
  70.7 1.7 %fusion.75 = (f32[256]{0:T(256)}, bf16[256,784]{0,1:T(8,128)(2,1)}) fusion(pred[256,784]{0,1:T(8,128)(4,1)S(1)} %copy-done.8, bf16[784,512]{1,0:T(8,128)(2,1)S(1)} %copy-done.6, bf16[256,512]{1,0:T(8,128)(2,1)S(1)} %copy-done.7), kind=kOutput, calls=%fused_computation.136 | convolution fusion | flops 26291968 | bytes 869376 | tf_op jit(solution)/shard_map/dot_general | solution.py:47
  72.4 1.7 %fusion.76 = (f32[256]{0:T(256)}, bf16[256,784]{0,1:T(8,128)(2,1)}) fusion(pred[256,784]{0,1:T(8,128)(4,1)S(1)} %copy-done.8, bf16[784,512]{1,0:T(8,128)(2,1)S(1)} %copy-done.6, bf16[256,512]{1,0:T(8,128)(2,1)S(1)} %copy-done.7), kind=kOutput, calls=%fused_computation.137 | convolution fusion | flops 26291968 | bytes 869376 | tf_op jit(solution)/shard_map/dot_general | solution.py:47
  74.1 1.8 %fusion.77 = (f32[256]{0:T(256)}, bf16[256,784]{0,1:T(8,128)(2,1)}) fusion(pred[256,784]{0,1:T(8,128)(4,1)S(1)} %copy-done.8, bf16[784,512]{1,0:T(8,128)(2,1)S(1)} %copy-done.6, bf16[256,512]{1,0:T(8,128)(2,1)S(1)} %copy-done.7), kind=kOutput, calls=%fused_computation.138 | convolution fusion | flops 26291968 | bytes 869376 | tf_op jit(solution)/shard_map/dot_general | solution.py:47
  78.1 2.1 %reshape.144 = bf16[784,512]{1,0:T(8,128)(2,1)} reshape(bf16[28,28,512]{2,1,0:T(8,128)(2,1)} %get-tuple-element.5) | data formatting | bytes 1605632 | tf_op jit(solution)/shard_map/reshape | solution.py:75
  81.7 1.5 %fusion.21 = bf16[256,512]{0,1:T(8,128)(2,1)S(1)} fusion(bf16[256,512]{0,1:T(8,128)(2,1)S(1)} %fusion.19, bf16[256,784]{0,1:T(8,128)(2,1)} %get-tuple-element.30, bf16[784,512]{1,0:T(8,128)(2,1)} %reshape.144, f32[256]{0:T(256)} %get-tuple-element.29), kind=kOutput, calls=%fused_computation.52 | convolution fusion | flops 25722880 | bytes 635904 | tf_op jit(solution)/shard_map/dot_general | solution.py:55
  90.5 2.7 %collective-permute-start.5 = (bf16[1,16,2048]{2,1,0:T(8,128)(2,1)S(1)}, bf16[1,16,2048]{2,1,0:T(8,128)(2,1)S(1)}, u32[]{:S(2)}, u32[]{:S(2)}) collective-permute-start(bf16[1,16,2048]{2,1,0:T(8,128)(2,1)S(1)} %get-tuple-element.13), channel_id=1, source_target_pairs={{16,0},{32,16},{48,32},{64,48},{80,64},{96,80},{112,96},{128,112},... | collective-permute-start | bytes 196616 | tf_op jit(solution)/shard_map/ppermute | solution.py:22
  93.3 1.8 %copy.34 = bf16[16,16,2048]{2,0,1:T(8,128)(2,1)S(1)} copy(bf16[16,16,2048]{2,1,0:T(8,128)(2,1)} %bitcast.44) | data formatting | bytes 2097152 | tf_op jit(solution)/shard_map/reshape | solution.py:122
  95.2 3.8 %collective-permute-done.4 = bf16[1,16,2048]{2,1,0:T(8,128)(2,1)S(1)} collective-permute-done((bf16[1,16,2048]{2,1,0:T(8,128)(2,1)S(1)}, bf16[1,16,2048]{2,1,0:T(8,128)(2,1)S(1)}, u32[]{:S(2)}, u32[]{:S(2)}) %collective-permute-start.4) | collective-permute-done | bytes 65568 | tf_op jit(solution)/shard_map/ppermute | solution.py:21
  99.2 9.7 %collective-permute-start.7 = (bf16[18,1,2048]{2,0,1:T(8,128)(2,1)S(1)}, bf16[18,1,2048]{2,0,1:T(8,128)(2,1)S(1)}, u32[]{:S(2)}, u32[]{:S(2)}) collective-permute-start(bf16[18,1,2048]{2,0,1:T(8,128)(2,1)S(1)} %get-tuple-element.11), channel_id=1, source_target_pairs={{1,0},{2,1},{3,2},{4,3},{5,4},{6,5},{7,6},{8,7},{9,8},{10,9},{11,1... | collective-permute-start | bytes 221192 | tf_op jit(solution)/shard_map/ppermute | solution.py:22
  109.0 2.2 %collective-permute-done.7 = bf16[18,1,2048]{2,0,1:T(8,128)(2,1)S(1)} collective-permute-done((bf16[18,1,2048]{2,0,1:T(8,128)(2,1)S(1)}, bf16[18,1,2048]{2,0,1:T(8,128)(2,1)S(1)}, u32[]{:S(2)}, u32[]{:S(2)}) %collective-permute-start.7) | collective-permute-done | bytes 73760 | tf_op jit(solution)/shard_map/ppermute | solution.py:22
  111.2 6.0 %collective-permute-done.6 = bf16[18,1,2048]{2,0,1:T(8,128)(2,1)S(1)} collective-permute-done((bf16[18,1,2048]{2,0,1:T(8,128)(2,1)S(1)}, bf16[18,1,2048]{2,0,1:T(8,128)(2,1)S(1)}, u32[]{:S(2)}, u32[]{:S(2)}) %collective-permute-start.6) | collective-permute-done | bytes 73760 | tf_op jit(solution)/shard_map/ppermute | solution.py:21
  118.1 7.1 %fusion.2 = bf16[16,16,2048]{2,0,1:T(8,128)(2,1)S(1)} fusion(bf16[18,18,2048]{2,0,1:T(8,128)(2,1)S(1)} %maximum_select_fusion, f32[2048]{0:T(1024)S(1)} %bitcast.52, f32[2048]{0:T(1024)S(1)} %bitcast.53, f32[2048]{0:T(1024)S(1)} %bitcast.46, f32[2048]{0:T(1024)S(1)} %bitcast.47, f32[2048]{0:T(1024)S(1)} %bitcast.48, f32[2048]{0:T(1024)S(1)} %bitcast.49, ...), kind=kLoop, calls=%fused_computation.4 | loop fusion | flops 47710208 | bytes 10559488 | tf_op jit(solution)/shard_map/convert_element_type | solution.py:137
  125.2 1.5 %copy.36 = bf16[16,16,2048]{2,1,0:T(8,128)(2,1)} copy(bf16[16,16,2048]{2,0,1:T(8,128)(2,1)S(1)} %fusion.2) | data formatting | bytes 2097152 | tf_op jit(solution)/shard_map/convert_element_type | solution.py:137
  (92 shorter events, 28.8 us)
Async XLA Ops:
  0.0 4.0 %copy-start = (bf16[1024,1536]{1,0:T(8,128)(2,1)S(1)}, bf16[1024,1536]{1,0:T(8,128)(2,1)}, u32[]{:S(2)}) copy-start(bf16[1024,1536]{1,0:T(8,128)(2,1)} %param.10) | copy-start | bytes 9437188
  5.0 1.2 copy-start.2
  6.3 6.8 %copy-start.10 = (f32[8]{0:T(128)S(1)}, f32[8]{0:T(128)}, u32[]{:S(2)}) copy-start(f32[8]{0:T(128)} %param.11) | copy-start | bytes 100
  25.7 5.0 %collective-permute-start.1 = (bf16[6,16,1024]{2,1,0:T(8,128)(2,1)}, bf16[6,16,1024]{2,1,0:T(8,128)(2,1)}, u32[]{:S(2)}, u32[]{:S(2)}) collective-permute-start(bf16[6,16,1024]{2,1,0:T(8,128)(2,1)} %get-tuple-element.17), channel_id=1, source_target_pairs={{16,0},{32,16},{48,32},{64,48},{80,64},{96,80},{112,96},{128,112},... | collective-permute-start | bytes 589832 | tf_op jit(solution)/shard_map/ppermute | solution.py:22
  27.1 7.5 %collective-permute-start = (bf16[6,16,1024]{2,1,0:T(8,128)(2,1)}, bf16[6,16,1024]{2,1,0:T(8,128)(2,1)}, u32[]{:S(2)}, u32[]{:S(2)}) collective-permute-start(bf16[6,16,1024]{2,1,0:T(8,128)(2,1)} %get-tuple-element.16), channel_id=1, source_target_pairs={{0,16},{16,32},{32,48},{48,64},{64,80},{80,96},{96,112},{112,128},... | collective-permute-start | bytes 589832 | tf_op jit(solution)/shard_map/ppermute | solution.py:21
  37.0 16.3 %collective-permute-start.3 = (bf16[28,6,1024]{2,1,0:T(8,128)(2,1)}, bf16[28,6,1024]{2,1,0:T(8,128)(2,1)}, u32[]{:S(2)}, u32[]{:S(2)}) collective-permute-start(bf16[28,6,1024]{2,1,0:T(8,128)(2,1)} %get-tuple-element.15), channel_id=1, source_target_pairs={{1,0},{2,1},{3,2},{4,3},{5,4},{6,5},{7,6},{8,7},{9,8},{10,9},{11,1... | collective-permute-start | bytes 1032200 | tf_op jit(solution)/shard_map/ppermute | solution.py:22
  45.1 12.4 %collective-permute-start.2 = (bf16[28,6,1024]{2,1,0:T(8,128)(2,1)}, bf16[28,6,1024]{2,1,0:T(8,128)(2,1)}, u32[]{:S(2)}, u32[]{:S(2)}) collective-permute-start(bf16[28,6,1024]{2,1,0:T(8,128)(2,1)} %get-tuple-element.14), channel_id=1, source_target_pairs={{0,1},{1,2},{2,3},{3,4},{4,5},{5,6},{6,7},{7,8},{8,9},{9,10},{10,1... | collective-permute-start | bytes 1032200 | tf_op jit(solution)/shard_map/ppermute | solution.py:21
  59.9 3.6 %copy-start.7 = (bf16[256,512]{1,0:T(8,128)(2,1)S(1)}, bf16[256,512]{1,0:T(8,128)(2,1)}, u32[]{:S(2)}) copy-start(bf16[256,512]{1,0:T(8,128)(2,1)} %get-tuple-element.7) | copy-start | bytes 786436
  63.4 5.6 %copy-start.6 = (bf16[784,512]{1,0:T(8,128)(2,1)S(1)}, bf16[784,512]{1,0:T(8,128)(2,1)}, u32[]{:S(2)}) copy-start(bf16[784,512]{1,0:T(8,128)(2,1)} %reshape.143) | copy-start | bytes 2408452
  63.4 5.6 %copy-start.8 = (pred[256,784]{0,1:T(8,128)(4,1)S(1)}, pred[256,784]{0,1:T(8,128)(4,1)}, u32[]{:S(2)}) copy-start(pred[256,784]{0,1:T(8,128)(4,1)} %copy.25) | copy-start | bytes 602116
  78.1 6.6 %copy-start.17 = (bf16[256,784]{0,1:T(8,128)(2,1)S(1)}, bf16[256,784]{0,1:T(8,128)(2,1)}, u32[]{:S(2)}) copy-start(bf16[256,784]{0,1:T(8,128)(2,1)} %get-tuple-element.34) | copy-start | bytes 1204228
  80.2 4.4 %copy-start.5 = (bf16[784,512]{1,0:T(8,128)(2,1)S(1)}, bf16[784,512]{1,0:T(8,128)(2,1)}, u32[]{:S(2)}) copy-start(bf16[784,512]{1,0:T(8,128)(2,1)} %reshape.144) | copy-start | bytes 2408452
  80.2 4.5 %copy-start.20 = (f32[256]{0:T(256)S(1)}, f32[256]{0:T(256)}, u32[]{:S(2)}) copy-start(f32[256]{0:T(256)} %get-tuple-element.33) | copy-start | bytes 3076
  80.2 4.8 %copy-start.16 = (bf16[256,784]{0,1:T(8,128)(2,1)S(1)}, bf16[256,784]{0,1:T(8,128)(2,1)}, u32[]{:S(2)}) copy-start(bf16[256,784]{0,1:T(8,128)(2,1)} %get-tuple-element.36) | copy-start | bytes 1204228
  80.2 4.8 %copy-start.19 = (f32[256]{0:T(256)S(1)}, f32[256]{0:T(256)}, u32[]{:S(2)}) copy-start(f32[256]{0:T(256)} %get-tuple-element.35) | copy-start | bytes 3076
  80.2 5.1 %copy-start.15 = (bf16[256,784]{0,1:T(8,128)(2,1)S(1)}, bf16[256,784]{0,1:T(8,128)(2,1)}, u32[]{:S(2)}) copy-start(bf16[256,784]{0,1:T(8,128)(2,1)} %get-tuple-element.38) | copy-start | bytes 1204228
  80.2 5.1 %copy-start.18 = (f32[256]{0:T(256)S(1)}, f32[256]{0:T(256)}, u32[]{:S(2)}) copy-start(f32[256]{0:T(256)} %get-tuple-element.37) | copy-start | bytes 3076
  81.7 4.0 %copy-start.14 = (bf16[256,784]{0,1:T(8,128)(2,1)S(1)}, bf16[256,784]{0,1:T(8,128)(2,1)}, u32[]{:S(2)}) copy-start(bf16[256,784]{0,1:T(8,128)(2,1)} %get-tuple-element.40) | copy-start | bytes 1204228
  83.2 2.7 %copy-start.13 = (bf16[256,784]{0,1:T(8,128)(2,1)S(1)}, bf16[256,784]{0,1:T(8,128)(2,1)}, u32[]{:S(2)}) copy-start(bf16[256,784]{0,1:T(8,128)(2,1)} %get-tuple-element.42) | copy-start | bytes 1204228
  84.7 1.7 %copy-start.1 = (bf16[16,16,1024]{2,1,0:T(8,128)(2,1)S(1)}, bf16[16,16,1024]{2,1,0:T(8,128)(2,1)}, u32[]{:S(2)}) copy-start(bf16[16,16,1024]{2,1,0:T(8,128)(2,1)} %param.8) | copy-start | bytes 1572868
  84.7 1.7 %copy-start.4 = (bf16[512,1024]{1,0:T(8,128)(2,1)S(1)}, bf16[512,1024]{1,0:T(8,128)(2,1)}, u32[]{:S(2)}) copy-start(bf16[512,1024]{1,0:T(8,128)(2,1)} %param.12) | copy-start | bytes 3145732
  86.0 2.2 %copy-start.11 = (bf16[1024,2048]{1,0:T(8,128)(2,1)S(1)}, bf16[1024,2048]{1,0:T(8,128)(2,1)}, u32[]{:S(2)}) copy-start(bf16[1024,2048]{1,0:T(8,128)(2,1)} %param.14) | copy-start | bytes 12582916
  86.4 1.9 %copy-start.12 = (f32[1024]{0:T(1024)S(1)}, f32[1024]{0:T(1024)}, u32[]{:S(2)}) copy-start(f32[1024]{0:T(1024)} %param.13) | copy-start | bytes 12292
  88.2 5.0 %copy-start.9 = (f32[3,3,2048]{2,1,0:T(4,128)S(1)}, f32[3,3,2048]{2,1,0:T(4,128)}, u32[]{:S(2)}) copy-start(f32[3,3,2048]{2,1,0:T(4,128)} %param.15) | copy-start | bytes 221188
  89.6 1.0 copy-start.3
  90.5 4.6 %collective-permute-start.5 = (bf16[1,16,2048]{2,1,0:T(8,128)(2,1)S(1)}, bf16[1,16,2048]{2,1,0:T(8,128)(2,1)S(1)}, u32[]{:S(2)}, u32[]{:S(2)}) collective-permute-start(bf16[1,16,2048]{2,1,0:T(8,128)(2,1)S(1)} %get-tuple-element.13), channel_id=1, source_target_pairs={{16,0},{32,16},{48,32},{64,48},{80,64},{96,80},{112,96},{128,112},... | collective-permute-start | bytes 196616 | tf_op jit(solution)/shard_map/ppermute | solution.py:22
  93.2 5.8 %collective-permute-start.4 = (bf16[1,16,2048]{2,1,0:T(8,128)(2,1)S(1)}, bf16[1,16,2048]{2,1,0:T(8,128)(2,1)S(1)}, u32[]{:S(2)}, u32[]{:S(2)}) collective-permute-start(bf16[1,16,2048]{2,1,0:T(8,128)(2,1)S(1)} %get-tuple-element.12), channel_id=1, source_target_pairs={{0,16},{16,32},{32,48},{48,64},{64,80},{80,96},{96,112},{112,128},... | collective-permute-start | bytes 196616 | tf_op jit(solution)/shard_map/ppermute | solution.py:21
  99.2 11.9 %collective-permute-start.7 = (bf16[18,1,2048]{2,0,1:T(8,128)(2,1)S(1)}, bf16[18,1,2048]{2,0,1:T(8,128)(2,1)S(1)}, u32[]{:S(2)}, u32[]{:S(2)}) collective-permute-start(bf16[18,1,2048]{2,0,1:T(8,128)(2,1)S(1)} %get-tuple-element.11), channel_id=1, source_target_pairs={{1,0},{2,1},{3,2},{4,3},{5,4},{6,5},{7,6},{8,7},{9,8},{10,9},{11,1... | collective-permute-start | bytes 221192 | tf_op jit(solution)/shard_map/ppermute | solution.py:22
  108.9 8.2 %collective-permute-start.6 = (bf16[18,1,2048]{2,0,1:T(8,128)(2,1)S(1)}, bf16[18,1,2048]{2,0,1:T(8,128)(2,1)S(1)}, u32[]{:S(2)}, u32[]{:S(2)}) collective-permute-start(bf16[18,1,2048]{2,0,1:T(8,128)(2,1)S(1)} %get-tuple-element.10), channel_id=1, source_target_pairs={{0,1},{1,2},{2,3},{3,4},{4,5},{5,6},{6,7},{7,8},{8,9},{9,10},{10,1... | collective-permute-start | bytes 221192 | tf_op jit(solution)/shard_map/ppermute | solution.py:21
where the time goes:
time: 127 us
  local copies, waits for them, and re-layouts  31 us (24%)
  other arithmetic  25.9 us (20%)
  waiting for transfers between devices  23.8 us (19%)
  matrix products  23.4 us (18%)
  starting transfers between devices  22.1 us (17%)
    ppermute x4, starting transfers between devices, with_halo(): after = lax.ppermute(leading, axis, down)  22.1 us
    ppermute x4, waiting for transfers between devices, with_halo(): before = lax.ppermute(last, axis, up)  18.1 us
    dot_general x8, matrix products, strip_attend(): lax.dot_general(query_block[:, lower:lower + HEAD_DIM], key_block[:, lowe...  14.6 us
    convert_element_type x1, other arithmetic, on_device(): return jax.nn.gelu(filtered, approximate=False).astype(jnp.bfloat16)  7.08 us
    mul x6, local copies, waits for them, and re-layouts, heads_norm(): vectors * lax.rsqrt(jnp.sum(vectors * vectors, -1, keepdims=True) + 1e-06)  6.61 us
    and x2, local copies, waits for them, and re-layouts, attend(): row_ok[:, None, :, None] & col_ok[None, :, None, :]  6.58 us
    dot_general x8, matrix products, strip_attend(): jnp.dot(weights.astype(jnp.bfloat16), value_block[:, lower:lower + HEAD_D...  5.9 us
    ppermute x4, waiting for transfers between devices, with_halo(): after = lax.ppermute(leading, axis, down)  5.73 us
  transfers between devices with their start and end apart: 8, of which 6 were waited for; matrix products, arithmetic and copies ran while one was open for 8% of the time, Pallas kernels for 0%

commit v1 on v0

v1 whole, which is shorter than its diff:
```python
import functools

import jax
import jax.numpy as jnp
from jax import lax
from jax.experimental import pallas as pl
from jax.experimental.pallas import tpu as pltpu
from jax.sharding import PartitionSpec as P

D = 1024
HEADS = 8
HEAD_DIM = 64
HID = 2048
RADIUS = 6
INNER = 512

SIDE = 16
REACH = RADIUS + 1
ROWS = SIDE + 2 * REACH
RING = SIDE + 2
HALF = RING * 8
EDGE = 32
STRIP = SIDE * REACH
CORNER = 64
CUT = STRIP - CORNER
KEYS_C = 512
KEYS_S = 256
PAIRS = HEADS // 2
TILE = 256
BF = jnp.bfloat16
F32 = jnp.float32
MESH = pl.DeviceIdType.MESH
FAR = -1e30

DOWN, UP, W_LOW, W_HIGH, E_LOW, E_HIGH, W_DOWN, W_UP, E_DOWN, E_UP = range(10)
L_TOK, L_GA, L_GF, L_TAPS, L_WK, L_WV, L_WQ, L_WO, L_WU = range(9)


def iota(shape, dim):
    return lax.broadcasted_iota(jnp.int32, shape, dim)


def div7(n):
    return (n * 9363) >> 16


def norm_rows(x, gain):
    centre = jnp.mean(x, -1, keepdims=True)
    moved = x - centre
    spread = jnp.mean(moved * moved, -1, keepdims=True)
    return moved * lax.rsqrt(spread + 1e-05) * gain


def gelu(x):
    size = jnp.abs(x)
    t = 1.0 / (1.0 + size * (0.3275911 * 0.7071067811865476))
    poly = 0.5 * 1.061405429
    for c in (-1.453152027, 1.421413741, -0.284496736, 0.254829592):
        poly = poly * t + 0.5 * c
    tail = poly * t * jnp.exp(x * x * -0.5)
    return jnp.maximum(x, 0.0) - size * tail


def kernel(
    tok, ga_h, wqkv_h, scale, wo_h, gf_h, wu_h, taps_h, out,
    ct, wt, et, xn, send_e, send_w, wk, wv, wq, wo, wu, ga, gf, taps,
    kc, vc, kw, vw, qc, qe, xres, acc_n, acc_d, bias_c, bias_s, bias_e,
    nf, hid_l, hid_r, ob, lsem, osem, ss, rs,
):
    lat, lon = lax.axis_index("lat"), lax.axis_index("lon")
    n_lat, n_lon = lax.axis_size("lat"), lax.axis_size("lon")
    east, west = lax.rem(lon + 1, n_lon), lax.rem(lon + n_lon - 1, n_lon)
    north_ok, south_ok = lat > 0, lat < n_lat - 1

    loc = [
        pltpu.make_async_copy(s, d, lsem.at[i])
        for i, (s, d) in enumerate((
            (tok, ct.at[pl.ds(REACH, SIDE)]),
            (ga_h, ga), (gf_h, gf), (taps_h, taps),
            (wqkv_h.at[:, pl.ds(INNER, INNER)], wk),
            (wqkv_h.at[:, pl.ds(2 * INNER, INNER)], wv),
            (wqkv_h.at[:, pl.ds(0, INNER)], wq),
            (wo_h, wo), (wu_h, wu),
        ))
    ]
    for c in loc:
        c.start()

    def remote(i, src, dst, device):
        return pltpu.make_async_remote_copy(
            src_ref=src, dst_ref=dst, send_sem=ss.at[i], recv_sem=rs.at[i],
            device_id=device, device_id_type=MESH,
        )

    below, above = (lat + 1, lon), (lat - 1, lon)
    to_e, to_w = (lat, east), (lat, west)
    low, high = pl.ds(CUT, CORNER), pl.ds(0, CUT)
    low_d, high_d = pl.ds(CORNER + CUT, CORNER), pl.ds(CORNER, CUT)
    top_d, bot_d = pl.ds(0, CORNER), pl.ds(CORNER + STRIP, CORNER)
    first_d = pl.ds(CORNER, CORNER)
    rem = [
        remote(DOWN, tok.at[pl.ds(SIDE - REACH, REACH)], ct.at[pl.ds(0, REACH)], below),
        remote(UP, tok.at[pl.ds(0, REACH)], ct.at[pl.ds(REACH + SIDE, REACH)], above),
        remote(W_LOW, send_e.at[low], wt.at[low_d], to_e),
        remote(W_HIGH, send_e.at[high], wt.at[high_d], to_e),
        remote(E_LOW, send_w.at[low], et.at[low_d], to_w),
        remote(E_HIGH, send_w.at[high], et.at[high_d], to_w),
        remote(W_DOWN, wt.at[low_d], wt.at[top_d], below),
        remote(W_UP, wt.at[first_d], wt.at[bot_d], above),
        remote(E_DOWN, et.at[low_d], et.at[top_d], below),
        remote(E_UP, et.at[first_d], et.at[bot_d], above),
    ]
    goes_south, goes_north = (DOWN, W_DOWN, E_DOWN), (UP, W_UP, E_UP)

    def start(i):
        if i in goes_south:
            pl.when(south_ok)(rem[i].start)
        elif i in goes_north:
            pl.when(north_ok)(rem[i].start)
        else:
            rem[i].start()

    def arrived(i):
        if i in goes_south:
            pl.when(north_ok)(rem[i].wait_recv)
        elif i in goes_north:
            pl.when(south_ok)(rem[i].wait_recv)
        else:
            rem[i].wait_recv()

    def sent(i):
        if i in goes_south:
            pl.when(south_ok)(rem[i].wait_send)
        elif i in goes_north:
            pl.when(north_ok)(rem[i].wait_send)
        else:
            rem[i].wait_send()

    barrier = pltpu.get_barrier_semaphore()
    for device in (to_e, to_w):
        pl.semaphore_signal(barrier, inc=1, device_id=device, device_id_type=MESH)

    @pl.when(south_ok)
    def _():
        pl.semaphore_signal(barrier, inc=1, device_id=below, device_id_type=MESH)

    @pl.when(north_ok)
    def _():
        pl.semaphore_signal(barrier, inc=1, device_id=above, device_id_type=MESH)

    ct[ROWS:, :, :] = jnp.zeros((32 - ROWS, SIDE, D), BF)
    for strip in (wt, et):
        strip[2 * CORNER + STRIP :, :] = jnp.zeros((KEYS_S - 2 * CORNER - STRIP, D), BF)

    @pl.when(lat == 0)
    def _():
        ct[:REACH, :, :] = jnp.zeros((REACH, SIDE, D), BF)
        for strip in (wt, et):
            strip[:CORNER, :] = jnp.zeros((CORNER, D), BF)

    @pl.when(lat == n_lat - 1)
    def _():
        ct[REACH + SIDE : ROWS, :, :] = jnp.zeros((REACH, SIDE, D), BF)
        for strip in (wt, et):
            strip[CORNER + STRIP : 2 * CORNER + STRIP, :] = jnp.zeros((CORNER, D), BF)

    loc[L_TOK].wait()
    mine = ct[REACH : REACH + SIDE].reshape(SIDE * SIDE, D)
    slot, source = iota((STRIP, SIDE * SIDE), 0), iota((STRIP, SIDE * SIDE), 1)
    origin = div7(slot) * (SIDE - REACH) + slot

    def pack(offset):
        pick = jnp.where(source == origin + offset, 1.0, 0.0).astype(BF)
        return jnp.dot(pick, mine, preferred_element_type=F32).astype(BF)

    send_e[...] = pack(SIDE - REACH)
    send_w[...] = pack(0)

    @pl.when(south_ok & north_ok)
    def _():
        pl.semaphore_wait(barrier, 4)

    @pl.when(jnp.logical_not(south_ok & north_ok))
    def _():
        pl.semaphore_wait(barrier, 3)

    for i in (W_LOW, W_HIGH, DOWN, UP, E_LOW, E_HIGH):
        start(i)

    def bias(q_row, q_col, k_row, k_col):
        place = lat * SIDE + k_row
        k_row = jnp.where((place >= 0) & (place < n_lat * SIDE), k_row, 1000)
        near = (jnp.abs(k_row - q_row) <= RADIUS) & (jnp.abs(k_col - q_col) <= RADIUS)
        return jnp.where(near, 0.0, FAR)

    m = iota((2 * HALF, 1), 0)
    right = jnp.where(m >= HALF, 1, 0)
    qc_row = ((m - right * HALF) >> 3) - 1
    qc_col = (m & 7) + 8 * right
    n = iota((1, KEYS_C), 1)
    kc_row = jnp.where(n < ROWS * SIDE, (n >> 4) - REACH, 1000)
    kc_col = n & 15
    bias_c[...] = bias(qc_row, qc_col, kc_row, kc_col)
    j = iota((1, KEYS_S), 1)
    ks_row7 = div7(j + 6)
    ks_row = jnp.where(j < 2 * CORNER + STRIP, ks_row7 - 10, 1000)
    ks_col = j + 6 - 7 * ks_row7
    e = iota((EDGE, 1), 0)
    h = iota((HALF, 1), 0)
    main_row, main_col = (h >> 3) - 1, h & 7
    for side, (first_q, edge_q, first_k) in enumerate(((0, -1, -REACH), (8, SIDE, SIDE))):
        bias_s[side, :HALF, :] = bias(main_row, main_col + first_q, ks_row, ks_col + first_k)
        bias_s[side, HALF:, :] = bias(e - 1, edge_q, ks_row, ks_col + first_k)
        bias_e[side] = bias(e - 1, edge_q, kc_row, kc_col)

    lane = iota((1, INNER), 1)
    factor = jnp.zeros((1, INNER), F32)
    for head in range(HEADS):
        factor = jnp.where((lane >> 6) == head, scale[head], factor)
    block = jnp.where(
        (iota((TILE, TILE), 0) >> 6) == (iota((TILE, TILE), 1) >> 6), 1.0, 0.0
    ).astype(BF)
    first_head = (iota((1, 128), 1) < HEAD_DIM)

    for vv in (vc, vw):
        vv[:, :, 128:] = jnp.ones((PAIRS, vv.shape[1], 128), BF)

    def unit(x):
        square = x * x
        top = square.astype(BF)
        rest = (square - top.astype(F32)).astype(BF)
        total = jnp.dot(top, block, preferred_element_type=F32) + jnp.dot(
            rest, block, preferred_element_type=F32
        )
        return x * lax.rsqrt(total + 1e-06)

    def keys_values(x, rows, k_dst, v_dst):
        for t in range(2):
            cols = pl.ds(t * TILE, TILE)
            keys = jnp.dot(x, wk[:, cols], preferred_element_type=F32)
            k_dst[rows, cols] = unit(keys).astype(BF)
        for t in range(2):
            cols = pl.ds(t * TILE, TILE)
            values = jnp.dot(x, wv[:, cols], preferred_element_type=F32).astype(BF)
            v_dst[2 * t, rows, :128] = values[:, :128]
            v_dst[2 * t + 1, rows, :128] = values[:, 128:]

    def attend(q, rows, k_src, v_src, bias_ref, take):
        count = q.shape[0]
        for p in range(PAIRS):
            cols = pl.ds(128 * p, 128)
            qp = q[:, 128 * p : 128 * p + 128]
            zero = jnp.zeros_like(qp)
            both = jnp.concatenate(
                [jnp.where(first_head, qp, zero), jnp.where(first_head, zero, qp)], 0
            )
            scores = lax.dot_general(
                both, k_src[:, cols], (((1,), (1,)), ((), ())), preferred_element_type=F32
            )
            term = bias_ref[...]
            weights = jnp.concatenate(
                [
                    jnp.exp(scores[:count] + term).astype(BF),
                    jnp.exp(scores[count:] + term).astype(BF),
                ],
                0,
            )
            summed = jnp.dot(weights, v_src[p], preferred_element_type=F32)
            take(
                cols,
                jnp.where(first_head, summed[:count, :128], summed[count:, :128]),
                jnp.where(first_head, summed[:count, 128:], summed[count:, 128:]),
            )

    loc[L_GA].wait()
    gain = ga[...]
    own = pl.ds(REACH * SIDE, SIDE * SIDE)
    xn[own, :] = norm_rows(mine.astype(F32), gain).astype(BF)
    loc[L_WK].wait()
    loc[L_WV].wait()
    keys_values(xn[own, :], own, kc, vc)

    for i, first, count in ((DOWN, 0, REACH), (UP, REACH + SIDE, 32 - REACH - SIDE)):
        arrived(i)
        rows = pl.ds(first * SIDE, count * SIDE)
        x = ct[first : first + count].reshape(count * SIDE, D).astype(F32)
        xn[rows, :] = norm_rows(x, gain).astype(BF)
        keys_values(xn[rows, :], rows, kc, vc)

    def halves(x):
        x = x.reshape(RING, 2, 8, x.shape[-1])
        return [x[:, s].reshape(HALF, x.shape[-1]) for s in range(2)]

    ring = pl.ds((REACH - 1) * SIDE, RING * SIDE)
    for s, part in enumerate(halves(ct[REACH - 1 : REACH + SIDE + 1].reshape(RING * SIDE, D).astype(F32))):
        xres[s * HALF : (s + 1) * HALF, :] = part
    loc[L_WQ].wait()
    for t in range(2):
        cols = pl.ds(t * TILE, TILE)
        q = jnp.dot(xn[ring, :], wq[:, cols], preferred_element_type=F32)
        q = unit(q) * factor[:, t * TILE : (t + 1) * TILE]
        for s, part in enumerate(halves(q)):
            qc[s * HALF : (s + 1) * HALF, cols] = part.astype(BF)

    arrived(W_LOW)
    start(W_DOWN)
    arrived(W_HIGH)
    start(W_UP)

    def keep(cols, num, den):
        acc_n[: 2 * HALF, cols] = num
        acc_d[: 2 * HALF, cols] = den

    attend(qc[...], None, kc, vc, bias_c, keep)

    loc[L_GF].wait()
    loc[L_TAPS].wait()
    loc[L_WO].wait()
    loc[L_WU].wait()
    edge_rows = pl.ds(2 * HALF, EDGE)

    def side_attention(side, strip):
        everything = pl.ds(0, KEYS_S)
        xs = norm_rows(strip[...].astype(F32), gain).astype(BF)
        keys_values(xs, everything, kw, vw)
        slot, source = iota((EDGE, KEYS_S), 0), iota((EDGE, KEYS_S), 1)
        first = (CORNER + REACH - 1, CORNER)[side] - REACH
        pick = jnp.where((source == slot * REACH + first) & (slot < RING), 1.0, 0.0).astype(BF)
        edge = jnp.dot(pick, strip[...], preferred_element_type=F32)
        xe = norm_rows(edge, gain).astype(BF)
        for t in range(2):
            cols = pl.ds(t * TILE, TILE)
            q = jnp.dot(xe, wq[:, cols], preferred_element_type=F32)
            qe[HALF:, cols] = (unit(q) * factor[:, t * TILE : (t + 1) * TILE]).astype(BF)
        main = pl.ds(side * HALF, HALF)
        qe[:HALF, :] = qc[main, :]

        def first_edge(cols, num, den):
            acc_n[edge_rows, cols] = num
            acc_d[edge_rows, cols] = den

        attend(qe[HALF:, :], None, kc, vc, bias_e.at[side], first_edge)

        def add(cols, num, den):
            acc_n[main, cols] += num[:HALF]
            acc_d[main, cols] += den[:HALF]
            acc_n[edge_rows, cols] += num[HALF:]
            acc_d[edge_rows, cols] += den[HALF:]

        attend(qe[...], None, kw, vw, bias_s.at[side], add)
        return edge

    def attended(rows):
        return (acc_n[rows, :] / acc_d[rows, :]).astype(BF)

    def ffn_input(att, tokens, row_of):
        stream = tokens + jnp.dot(att, wo[...], preferred_element_type=F32)
        place = lat * SIDE + row_of - 1
        inside = (place >= 0) & (place < n_lat * SIDE)
        return jnp.where(inside, norm_rows(stream, gf[...]), 0.0).astype(BF)

    def up_project(count, hid):
        @pl.loop(0, HID // TILE)
        def _(t):
            cols = pl.ds(pl.multiple_of(t * TILE, TILE), TILE)
            hidden = jnp.dot(nf[:count, :], wu[:, cols], preferred_element_type=F32)
            hid[:count, cols] = hidden.astype(BF).astype(F32)

    sub = iota((8, TILE), 0)

    def filter_half(side, hid, west_row, east_row):
        @pl.loop(0, HID // TILE)
        def _(t):
            cols = pl.ds(pl.multiple_of(t * TILE, TILE), TILE)
            tap = [[taps[a, pl.ds(b, 1), cols] for b in range(3)] for a in range(3)]
            total = [None] * RING
            for g in range(RING):
                mid = hid[g * 8 : g * 8 + 8, cols]
                w_edge, e_edge = west_row(g, cols), east_row(g, cols)
                lower = jnp.where(sub == 0, w_edge, pltpu.roll(mid, 1, 0))
                upper = jnp.where(sub == 7, e_edge, pltpu.roll(mid, 7, 0))
                for a in range(3):
                    r = g - a
                    if 0 <= r < SIDE:
                        term = lower * tap[a][0] + mid * tap[a][1] + upper * tap[a][2]
                        total[r] = term if total[r] is None else total[r] + term
                if g >= 2:
                    r = g - 2
                    ob[r, side * 8 : side * 8 + 8, cols] = gelu(total[r]).astype(BF)

    arrived(W_DOWN)
    arrived(W_UP)
    edge = side_attention(0, wt)
    nf[:HALF, :] = ffn_input(attended(pl.ds(0, HALF)), xres[:HALF, :], h >> 3)
    nf[HALF : HALF + EDGE, :] = ffn_input(attended(edge_rows), edge, e)
    slot, source = iota((EDGE, HALF), 0), iota((EDGE, HALF), 1)
    pick = jnp.where((source == slot * 8) & (slot < RING), 1.0, 0.0).astype(BF)
    att = (acc_n[HALF : 2 * HALF, :] / acc_d[HALF : 2 * HALF, :]).astype(BF)
    att = jnp.dot(pick, att, preferred_element_type=F32).astype(BF)
    slot, source = iota((EDGE, KEYS_C), 0), iota((EDGE, KEYS_C), 1)
    pick = (source == (slot + REACH - 1) * SIDE + 8) & (slot < RING)
    pick = jnp.where(pick, 1.0, 0.0).astype(BF)
    tokens = jnp.dot(pick, ct[...].reshape(KEYS_C, D), preferred_element_type=F32)
    nf[HALF + EDGE :, :] = ffn_input(att, tokens, e)

    arrived(E_LOW)
    start(E_DOWN)
    up_project(HALF + 2 * EDGE, hid_l)
    arrived(E_HIGH)
    start(E_UP)
    filter_half(
        0, hid_l,
        lambda g, cols: hid_l[HALF + g : HALF + g + 1, cols],
        lambda g, cols: hid_l[HALF + EDGE + g : HALF + EDGE + g + 1, cols],
    )

    arrived(E_DOWN)
    arrived(E_UP)
    edge = side_attention(1, et)
    nf[:HALF, :] = ffn_input(attended(pl.ds(HALF, HALF)), xres[HALF : 2 * HALF, :], h >> 3)
    nf[HALF : HALF + EDGE, :] = ffn_input(attended(edge_rows), edge, e)
    up_project(HALF + EDGE, hid_r)
    filter_half(
        1, hid_r,
        lambda g, cols: hid_l[g * 8 + 7 : g * 8 + 8, cols],
        lambda g, cols: hid_r[HALF + g : HALF + g + 1, cols],
    )
    done = pltpu.make_async_copy(ob, out, osem.at[0])
    done.start()
    for i in range(len(rem)):
        sent(i)
    done.wait()


def on_device(tokens, gain_attn, w_qkv, logit_scale, w_out, gain_ffn, w_up, conv_taps):
    vm = pltpu.VMEM
    anywhere = pl.BlockSpec(memory_space=pl.ANY)
    return pl.pallas_call(
        kernel,
        out_shape=jax.ShapeDtypeStruct((SIDE, SIDE, HID), BF),
        in_specs=[anywhere] * 3 + [pl.BlockSpec(memory_space=pltpu.SMEM)] + [anywhere] * 4,
        out_specs=anywhere,
        scratch_shapes=[
            vm((32, SIDE, D), BF),
            vm((KEYS_S, D), BF),
            vm((KEYS_S, D), BF),
            vm((KEYS_C, D), BF),
            vm((STRIP, D), BF),
            vm((STRIP, D), BF),
            vm((D, INNER), BF),
            vm((D, INNER), BF),
            vm((D, INNER), BF),
            vm((INNER, D), BF),
            vm((D, HID), BF),
            vm((1, D), F32),
            vm((1, D), F32),
            vm((3, 3, HID), F32),
            vm((KEYS_C, INNER), BF),
            vm((PAIRS, KEYS_C, 256), BF),
            vm((KEYS_S, INNER), BF),
            vm((PAIRS, KEYS_S, 256), BF),
            vm((2 * HALF, INNER), BF),
            vm((HALF + EDGE, INNER), BF),
            vm((2 * HALF, D), F32),
            vm((2 * HALF + EDGE, INNER), F32),
            vm((2 * HALF + EDGE, INNER), F32),
            vm((2 * HALF, KEYS_C), F32),
            vm((2, HALF + EDGE, KEYS_S), F32),
            vm((2, EDGE, KEYS_C), F32),
            vm((HALF + 2 * EDGE, D), BF),
            vm((HALF + 2 * EDGE, HID), F32),
            vm((HALF + EDGE, HID), F32),
            vm((SIDE, SIDE, HID), BF),
            pltpu.SemaphoreType.DMA((9,)),
            pltpu.SemaphoreType.DMA((2,)),
            pltpu.SemaphoreType.DMA((10,)),
            pltpu.SemaphoreType.DMA((10,)),
        ],
        compiler_params=pltpu.CompilerParams(
            collective_id=0, has_side_effects=True, vmem_limit_bytes=60 * 2**20
        ),
        name="weather_block",
    )(
        tokens, gain_attn.reshape(1, D), w_qkv, logit_scale, w_out,
        gain_ffn.reshape(1, D), w_up, conv_taps,
    )


def solution(mesh):
    in_specs = (P("lat", "lon", None), P(), P(), P(), P(), P(), P(), P())
    return jax.shard_map(
        on_device, mesh=mesh, in_specs=in_specs, out_specs=P("lat", "lon", None), check_vma=False
    )
```

time: 127 us -> 43.9 us (0.35)
  the two profiles are of different devices: /device:TPU:0 before, /device:TPU:7 now
where the time goes in v1:
time: 43.9 us; the launch traced here: 43.8 us
  Pallas kernels  41.5 us (95%)
  local copies, waits for them, and re-layouts  2.3 us (5%)
    pallas_call x1, Pallas kernels, on_device(): pl.pallas_call(kernel, out_shape=jax.ShapeDtypeStruct((SIDE, SIDE, HID),...  41.5 us
    unnamed x1, local copies, waits for them, and re-layouts  2.3 us

profile of v1, /device:TPU:7, one launch (start us, length us, event | category | flops | bytes accessed | tf_op | source)
XLA Modules:
  0.0 43.8 jit_solution(16218072783325553336)
XLA Ops:
  0.0 41.5 %weather_block.1 = bf16[16,16,2048]{2,1,0:T(8,128)(2,1)} custom-call(bf16[16,16,1024]{2,1,0:T(8,128)(2,1)} %tok.1, f32[1,1024]{1,0:T(1,128)} %bitcast.2, bf16[1024,1536]{1,0:T(8,128)(2,1)} %wqkv_h.1, f32[8]{0:T(128)} %scale.1, bf16[512,1024]{1,0:T(8,128)(2,1)} %wo_h.1, f32[1,1024]{1,0:T(1,128)} %bitcast.3, bf16[1024,2048]{1,0:T(8,128)(2,1)} %wu_h.1, ...), custom_call_target="tpu_custom_call" | custom-call | tf_op jit(solution)/shard_map/weather_block/pallas_call | solution.py:438
  41.5 2.3 %copy.10 = bf16[16,16,2048]{2,1,0:T(8,128)(2,1)} copy(bf16[16,16,2048]{2,1,0:T(8,128)(2,1)} %weather_block.1) | data formatting | bytes 2097152

commit v2 on v1

--- a/solution.py
+++ b/solution.py
@@ -184,8 +184,22 @@
     def _():
         pl.semaphore_wait(barrier, 3)
 
-    for i in (W_LOW, W_HIGH, DOWN, UP, E_LOW, E_HIGH):
-        start(i)
+    start(DOWN)
+    start(UP)
+    late = lon == n_lon - 1
+
+    @pl.when(late)
+    def _():
+        for i in (W_LOW, W_HIGH, E_LOW, E_HIGH):
+            start(i)
+
+    @pl.when(jnp.logical_not(late))
+    def _():
+        for i in (E_LOW, E_HIGH, W_LOW, W_HIGH):
+            start(i)
+
+    def follow(i):
+        pl.when(jnp.logical_not(late))(lambda: start(i))
 
     def bias(q_row, q_col, k_row, k_col):
         place = lat * SIDE + k_row
@@ -229,63 +243,80 @@
         square = x * x
         top = square.astype(BF)
         rest = (square - top.astype(F32)).astype(BF)
-        total = jnp.dot(top, block, preferred_element_type=F32) + jnp.dot(
-            rest, block, preferred_element_type=F32
-        )
-        return x * lax.rsqrt(total + 1e-06)
-
-    def keys_values(x, rows, k_dst, v_dst):
-        for t in range(2):
-            cols = pl.ds(t * TILE, TILE)
-            keys = jnp.dot(x, wk[:, cols], preferred_element_type=F32)
-            k_dst[rows, cols] = unit(keys).astype(BF)
-        for t in range(2):
-            cols = pl.ds(t * TILE, TILE)
-            values = jnp.dot(x, wv[:, cols], preferred_element_type=F32).astype(BF)
-            v_dst[2 * t, rows, :128] = values[:, :128]
-            v_dst[2 * t + 1, rows, :128] = values[:, 128:]
-
-    def attend(q, rows, k_src, v_src, bias_ref, take):
+        totals = []
+        for t in range(INNER // TILE):
+            cols = slice(t * TILE, (t + 1) * TILE)
+            totals.append(
+                jnp.dot(top[:, cols], block, preferred_element_type=F32)
+                + jnp.dot(rest[:, cols], block, preferred_element_type=F32)
+            )
+        return x * lax.rsqrt(jnp.concatenate(totals, 1) + 1e-06)
+
+    def keys_values(x, pieces, k_dst, v_dst):
+        keys = jnp.dot(x, wk[...], preferred_element_type=F32)
+        values = jnp.dot(x, wv[...], preferred_element_type=F32).astype(BF)
+        keys = unit(keys).astype(BF)
+        for first, start_row, count in pieces:
+            k_dst[start_row : start_row + count, :] = keys[first : first + count]
+            for p in range(PAIRS):
+                v_dst[p, start_row : start_row + count, :128] = values[
+                    first : first + count, 128 * p : 128 * p + 128
+                ]
+
+    def attend(q, k_src, v_src, bias_ref, take):
         count = q.shape[0]
+        scores = []
         for p in range(PAIRS):
-            cols = pl.ds(128 * p, 128)
             qp = q[:, 128 * p : 128 * p + 128]
             zero = jnp.zeros_like(qp)
             both = jnp.concatenate(
                 [jnp.where(first_head, qp, zero), jnp.where(first_head, zero, qp)], 0
             )
-            scores = lax.dot_general(
-                both, k_src[:, cols], (((1,), (1,)), ((), ())), preferred_element_type=F32
-            )
-            term = bias_ref[...]
+            scores.append(lax.dot_general(
+                both, k_src[:, 128 * p : 128 * p + 128], (((1,), (1,)), ((), ())),
+                preferred_element_type=F32,
+            ))
+        term = bias_ref[...]
+        for p in range(PAIRS):
             weights = jnp.concatenate(
                 [
-                    jnp.exp(scores[:count] + term).astype(BF),
-                    jnp.exp(scores[count:] + term).astype(BF),
+                    jnp.exp(scores[p][:count] + term).astype(BF),
+                    jnp.exp(scores[p][count:] + term).astype(BF),
                 ],
                 0,
             )
             summed = jnp.dot(weights, v_src[p], preferred_element_type=F32)
             take(
-                cols,
+                slice(128 * p, 128 * p + 128),
                 jnp.where(first_head, summed[:count, :128], summed[count:, :128]),
                 jnp.where(first_head, summed[:count, 128:], summed[count:, 128:]),
             )
 
     loc[L_GA].wait()
     gain = ga[...]
-    own = pl.ds(REACH * SIDE, SIDE * SIDE)
-    xn[own, :] = norm_rows(mine.astype(F32), gain).astype(BF)
+    own = REACH * SIDE
+    xn[own : own + SIDE * SIDE, :] = norm_rows(mine.astype(F32), gain).astype(BF)
     loc[L_WK].wait()
     loc[L_WV].wait()
-    keys_values(xn[own, :], own, kc, vc)
-
-    for i, first, count in ((DOWN, 0, REACH), (UP, REACH + SIDE, 32 - REACH - SIDE)):
-        arrived(i)
-        rows = pl.ds(first * SIDE, count * SIDE)
-        x = ct[first : first + count].reshape(count * SIDE, D).astype(F32)
-        xn[rows, :] = norm_rows(x, gain).astype(BF)
-        keys_values(xn[rows, :], rows, kc, vc)
+    keys_values(xn[own : own + SIDE * SIDE, :], ((0, own, SIDE * SIDE),), kc, vc)
+
+    arrived(DOWN)
+    arrived(UP)
+    tail_rows = (32 - REACH - SIDE) * SIDE
+    tail = own + SIDE * SIDE
+    x = jnp.concatenate(
+        [
+            ct[:REACH].reshape(own, D).astype(F32),
+            ct[REACH + SIDE :].reshape(tail_rows, D).astype(F32),
+        ],
+        0,
+    )
+    x = norm_rows(x, gain).astype(BF)
+    xn[:own, :] = x[:own]
+    xn[tail:, :] = x[own:]
+    keys_values(x, ((0, 0, own), (own, tail, tail_rows)), kc, vc)
+    arrived(E_LOW)
+    start(E_DOWN)
 
     def halves(x):
         x = x.reshape(RING, 2, 8, x.shape[-1])
@@ -295,51 +326,45 @@
     for s, part in enumerate(halves(ct[REACH - 1 : REACH + SIDE + 1].reshape(RING * SIDE, D).astype(F32))):
         xres[s * HALF : (s + 1) * HALF, :] = part
     loc[L_WQ].wait()
-    for t in range(2):
-        cols = pl.ds(t * TILE, TILE)
-        q = jnp.dot(xn[ring, :], wq[:, cols], preferred_element_type=F32)
-        q = unit(q) * factor[:, t * TILE : (t + 1) * TILE]
-        for s, part in enumerate(halves(q)):
-            qc[s * HALF : (s + 1) * HALF, cols] = part.astype(BF)
-
-    arrived(W_LOW)
-    start(W_DOWN)
-    arrived(W_HIGH)
-    start(W_UP)
+    q = unit(jnp.dot(xn[ring, :], wq[...], preferred_element_type=F32)) * factor
+    for s, part in enumerate(halves(q)):
+        qc[s * HALF : (s + 1) * HALF, :] = part.astype(BF)
 
     def keep(cols, num, den):
         acc_n[: 2 * HALF, cols] = num
         acc_d[: 2 * HALF, cols] = den
 
-    attend(qc[...], None, kc, vc, bias_c, keep)
-
-    loc[L_GF].wait()
-    loc[L_TAPS].wait()
-    loc[L_WO].wait()
-    loc[L_WU].wait()
-    edge_rows = pl.ds(2 * HALF, EDGE)
+    arrived(E_HIGH)
+    start(E_UP)
+    attend(qc[...], kc, vc, bias_c, keep)
+
+    edge_rows = slice(2 * HALF, 2 * HALF + EDGE)
+    strip_end = CORNER + STRIP
+
+    def side_middle(strip):
+        x = norm_rows(strip[CORNER:strip_end, :].astype(F32), gain).astype(BF)
+        keys_values(x, ((0, CORNER, STRIP),), kw, vw)
 
     def side_attention(side, strip):
-        everything = pl.ds(0, KEYS_S)
-        xs = norm_rows(strip[...].astype(F32), gain).astype(BF)
-        keys_values(xs, everything, kw, vw)
+        last = KEYS_S - strip_end
         slot, source = iota((EDGE, KEYS_S), 0), iota((EDGE, KEYS_S), 1)
         first = (CORNER + REACH - 1, CORNER)[side] - REACH
         pick = jnp.where((source == slot * REACH + first) & (slot < RING), 1.0, 0.0).astype(BF)
         edge = jnp.dot(pick, strip[...], preferred_element_type=F32)
+        x = jnp.concatenate([strip[:CORNER, :], strip[strip_end:, :]], 0).astype(F32)
+        x = norm_rows(x, gain).astype(BF)
+        keys_values(x, ((0, 0, CORNER), (CORNER, strip_end, last)), kw, vw)
         xe = norm_rows(edge, gain).astype(BF)
-        for t in range(2):
-            cols = pl.ds(t * TILE, TILE)
-            q = jnp.dot(xe, wq[:, cols], preferred_element_type=F32)
-            qe[HALF:, cols] = (unit(q) * factor[:, t * TILE : (t + 1) * TILE]).astype(BF)
-        main = pl.ds(side * HALF, HALF)
+        q = unit(jnp.dot(xe, wq[...], preferred_element_type=F32)) * factor
+        qe[HALF:, :] = q.astype(BF)
+        main = slice(side * HALF, side * HALF + HALF)
         qe[:HALF, :] = qc[main, :]
 
         def first_edge(cols, num, den):
             acc_n[edge_rows, cols] = num
             acc_d[edge_rows, cols] = den
 
-        attend(qe[HALF:, :], None, kc, vc, bias_e.at[side], first_edge)
+        attend(qe[HALF:, :], kc, vc, bias_e.at[side], first_edge)
 
         def add(cols, num, den):
             acc_n[main, cols] += num[:HALF]
@@ -347,7 +372,7 @@
             acc_n[edge_rows, cols] += num[HALF:]
             acc_d[edge_rows, cols] += den[HALF:]
 
-        attend(qe[...], None, kw, vw, bias_s.at[side], add)
+        attend(qe[...], kw, vw, bias_s.at[side], add)
         return edge
 
     def attended(rows):
@@ -360,15 +385,18 @@
         return jnp.where(inside, norm_rows(stream, gf[...]), 0.0).astype(BF)
 
     def up_project(count, hid):
-        @pl.loop(0, HID // TILE)
-        def _(t):
-            cols = pl.ds(pl.multiple_of(t * TILE, TILE), TILE)
+        for t in range(HID // 512):
+            cols = slice(t * 512, (t + 1) * 512)
             hidden = jnp.dot(nf[:count, :], wu[:, cols], preferred_element_type=F32)
             hid[:count, cols] = hidden.astype(BF).astype(F32)
 
     sub = iota((8, TILE), 0)
 
-    def filter_half(side, hid, west_row, east_row):
+    def block_out(t):
+        cols = pl.ds(pl.multiple_of(t * TILE, TILE), TILE)
+        return pltpu.make_async_copy(ob.at[:, :, cols], out.at[:, :, cols], osem.at[t])
+
+    def filter_half(side, hid, west_row, east_row, write):
         @pl.loop(0, HID // TILE)
         def _(t):
             cols = pl.ds(pl.multiple_of(t * TILE, TILE), TILE)
@@ -387,49 +415,57 @@
                 if g >= 2:
                     r = g - 2
                     ob[r, side * 8 : side * 8 + 8, cols] = gelu(total[r]).astype(BF)
+            if write:
+                block_out(t).start()
+
+    side_middle(et)
+    arrived(E_DOWN)
+    arrived(E_UP)
+    edge = side_attention(1, et)
+    arrived(W_LOW)
+    start(W_DOWN)
+    arrived(W_HIGH)
+    start(W_UP)
+    loc[L_GF].wait()
+    loc[L_TAPS].wait()
+    loc[L_WO].wait()
+    loc[L_WU].wait()
+    nf[:HALF, :] = ffn_input(attended(slice(HALF, 2 * HALF)), xres[HALF:, :], h >> 3)
+    nf[HALF : HALF + EDGE, :] = ffn_input(attended(edge_rows), edge, e)
+    slot, source = iota((EDGE, HALF), 0), iota((EDGE, HALF), 1)
+    pick = jnp.where((source == slot * 8 + 7) & (slot < RING), 1.0, 0.0).astype(BF)
+    att = jnp.dot(pick, attended(slice(0, HALF)), preferred_element_type=F32).astype(BF)
+    slot, source = iota((EDGE, KEYS_C), 0), iota((EDGE, KEYS_C), 1)
+    pick = (source == (slot + REACH - 1) * SIDE + 7) & (slot < RING)
+    pick = jnp.where(pick, 1.0, 0.0).astype(BF)
+    tokens = jnp.dot(pick, ct[...].reshape(KEYS_C, D), preferred_element_type=F32)
+    nf[HALF + EDGE :, :] = ffn_input(att, tokens, e)
+
+    up_project(HALF + 2 * EDGE, hid_r)
+    side_middle(wt)
+    filter_half(
+        1, hid_r,
+        lambda g, cols: hid_r[HALF + EDGE + g : HALF + EDGE + g + 1, cols],
+        lambda g, cols: hid_r[HALF + g : HALF + g + 1, cols],
+        False,
+    )
 
     arrived(W_DOWN)
     arrived(W_UP)
     edge = side_attention(0, wt)
-    nf[:HALF, :] = ffn_input(attended(pl.ds(0, HALF)), xres[:HALF, :], h >> 3)
+    nf[:HALF, :] = ffn_input(attended(slice(0, HALF)), xres[:HALF, :], h >> 3)
     nf[HALF : HALF + EDGE, :] = ffn_input(attended(edge_rows), edge, e)
-    slot, source = iota((EDGE, HALF), 0), iota((EDGE, HALF), 1)
-    pick = jnp.where((source == slot * 8) & (slot < RING), 1.0, 0.0).astype(BF)
-    att = (acc_n[HALF : 2 * HALF, :] / acc_d[HALF : 2 * HALF, :]).astype(BF)
-    att = jnp.dot(pick, att, preferred_element_type=F32).astype(BF)
-    slot, source = iota((EDGE, KEYS_C), 0), iota((EDGE, KEYS_C), 1)
-    pick = (source == (slot + REACH - 1) * SIDE + 8) & (slot < RING)
-    pick = jnp.where(pick, 1.0, 0.0).astype(BF)
-    tokens = jnp.dot(pick, ct[...].reshape(KEYS_C, D), preferred_element_type=F32)
-    nf[HALF + EDGE :, :] = ffn_input(att, tokens, e)
-
-    arrived(E_LOW)
-    start(E_DOWN)
-    up_project(HALF + 2 * EDGE, hid_l)
-    arrived(E_HIGH)
-    start(E_UP)
+    up_project(HALF + EDGE, hid_l)
     filter_half(
         0, hid_l,
         lambda g, cols: hid_l[HALF + g : HALF + g + 1, cols],
-        lambda g, cols: hid_l[HALF + EDGE + g : HALF + EDGE + g + 1, cols],
+        lambda g, cols: hid_r[g * 8 : g * 8 + 1, cols],
+        True,
     )
-
-    arrived(E_DOWN)
-    arrived(E_UP)
-    edge = side_attention(1, et)
-    nf[:HALF, :] = ffn_input(attended(pl.ds(HALF, HALF)), xres[HALF : 2 * HALF, :], h >> 3)
-    nf[HALF : HALF + EDGE, :] = ffn_input(attended(edge_rows), edge, e)
-    up_project(HALF + EDGE, hid_r)
-    filter_half(
-        1, hid_r,
-        lambda g, cols: hid_l[g * 8 + 7 : g * 8 + 8, cols],
-        lambda g, cols: hid_r[HALF + g : HALF + g + 1, cols],
-    )
-    done = pltpu.make_async_copy(ob, out, osem.at[0])
-    done.start()
     for i in range(len(rem)):
         sent(i)
-    done.wait()
+    for t in range(HID // TILE):
+        block_out(t).wait()
 
 
 def on_device(tokens, gain_attn, w_qkv, logit_scale, w_out, gain_ffn, w_up, conv_taps):
@@ -468,11 +504,11 @@
             vm((2, HALF + EDGE, KEYS_S), F32),
             vm((2, EDGE, KEYS_C), F32),
             vm((HALF + 2 * EDGE, D), BF),
+            vm((HALF + EDGE, HID), F32),
             vm((HALF + 2 * EDGE, HID), F32),
-            vm((HALF + EDGE, HID), F32),
             vm((SIDE, SIDE, HID), BF),
             pltpu.SemaphoreType.DMA((9,)),
-            pltpu.SemaphoreType.DMA((2,)),
+            pltpu.SemaphoreType.DMA((HID // TILE,)),
             pltpu.SemaphoreType.DMA((10,)),
             pltpu.SemaphoreType.DMA((10,)),
         ],

time: 43.9 us -> 38.7 us (0.88)
  the two profiles are of different devices: /device:TPU:7 before, /device:TPU:13 now
where the time goes in v2:
time: 38.7 us; the launch traced here: 38.6 us
  Pallas kernels  36.3 us (94%)
  local copies, waits for them, and re-layouts  2.3 us (6%)
    pallas_call x1, Pallas kernels, on_device(): pl.pallas_call(kernel, out_shape=jax.ShapeDtypeStruct((SIDE, SIDE, HID),...  36.3 us
    unnamed x1, local copies, waits for them, and re-layouts  2.3 us

profile of v2, /device:TPU:13, one launch (start us, length us, event | category | flops | bytes accessed | tf_op | source)
XLA Modules:
  0.0 38.6 jit_solution(6377916584677131456)
XLA Ops:
  0.0 36.3 %weather_block.1 = bf16[16,16,2048]{2,1,0:T(8,128)(2,1)} custom-call(bf16[16,16,1024]{2,1,0:T(8,128)(2,1)} %tok.1, f32[1,1024]{1,0:T(1,128)} %bitcast.2, bf16[1024,1536]{1,0:T(8,128)(2,1)} %wqkv_h.1, f32[8]{0:T(128)} %scale.1, bf16[512,1024]{1,0:T(8,128)(2,1)} %wo_h.1, f32[1,1024]{1,0:T(1,128)} %bitcast.3, bf16[1024,2048]{1,0:T(8,128)(2,1)} %wu_h.1, ...), custom_call_target="tpu_custom_call" | custom-call | tf_op jit(solution)/shard_map/weather_block/pallas_call | solution.py:474
  36.3 2.3 %copy.10 = bf16[16,16,2048]{2,1,0:T(8,128)(2,1)} copy(bf16[16,16,2048]{2,1,0:T(8,128)(2,1)} %weather_block.1) | data formatting | bytes 2097152

commit v3 on v2

--- a/solution.py
+++ b/solution.py
@@ -33,7 +33,7 @@
 FAR = -1e30
 
 DOWN, UP, W_LOW, W_HIGH, E_LOW, E_HIGH, W_DOWN, W_UP, E_DOWN, E_UP = range(10)
-L_TOK, L_GA, L_GF, L_TAPS, L_WK, L_WV, L_WQ, L_WO, L_WU = range(9)
+L_TOK, L_GA, L_GF, L_TAPS, L_WK, L_WV, L_WQ, L_WO, L_WU, L_SCALE = range(10)
 
 
 def iota(shape, dim):
@@ -62,10 +62,10 @@
 
 
 def kernel(
-    tok, ga_h, wqkv_h, scale, wo_h, gf_h, wu_h, taps_h, out,
+    tok, ga_h, wqkv_h, scale_h, wo_h, gf_h, wu_h, taps_h, out,
     ct, wt, et, xn, send_e, send_w, wk, wv, wq, wo, wu, ga, gf, taps,
     kc, vc, kw, vw, qc, qe, xres, acc_n, acc_d, bias_c, bias_s, bias_e,
-    nf, hid_l, hid_r, ob, lsem, osem, ss, rs,
+    nf, hid_l, hid_r, scale, lsem, ss, rs,
 ):
     lat, lon = lax.axis_index("lat"), lax.axis_index("lon")
     n_lat, n_lon = lax.axis_size("lat"), lax.axis_size("lon")
@@ -80,7 +80,7 @@
             (wqkv_h.at[:, pl.ds(INNER, INNER)], wk),
             (wqkv_h.at[:, pl.ds(2 * INNER, INNER)], wv),
             (wqkv_h.at[:, pl.ds(0, INNER)], wq),
-            (wo_h, wo), (wu_h, wu),
+            (wo_h, wo), (wu_h, wu), (scale_h, scale),
         ))
     ]
     for c in loc:
@@ -227,6 +227,7 @@
         bias_s[side, HALF:, :] = bias(e - 1, edge_q, ks_row, ks_col + first_k)
         bias_e[side] = bias(e - 1, edge_q, kc_row, kc_col)
 
+    loc[L_SCALE].wait()
     lane = iota((1, INNER), 1)
     factor = jnp.zeros((1, INNER), F32)
     for head in range(HEADS):
@@ -392,11 +393,7 @@
 
     sub = iota((8, TILE), 0)
 
-    def block_out(t):
-        cols = pl.ds(pl.multiple_of(t * TILE, TILE), TILE)
-        return pltpu.make_async_copy(ob.at[:, :, cols], out.at[:, :, cols], osem.at[t])
-
-    def filter_half(side, hid, west_row, east_row, write):
+    def filter_half(side, hid, west_row, east_row):
         @pl.loop(0, HID // TILE)
         def _(t):
             cols = pl.ds(pl.multiple_of(t * TILE, TILE), TILE)
@@ -414,9 +411,7 @@
                         total[r] = term if total[r] is None else total[r] + term
                 if g >= 2:
                     r = g - 2
-                    ob[r, side * 8 : side * 8 + 8, cols] = gelu(total[r]).astype(BF)
-            if write:
-                block_out(t).start()
+                    out[r, side * 8 : side * 8 + 8, cols] = gelu(total[r]).astype(BF)
 
     side_middle(et)
     arrived(E_DOWN)
@@ -447,7 +442,6 @@
         1, hid_r,
         lambda g, cols: hid_r[HALF + EDGE + g : HALF + EDGE + g + 1, cols],
         lambda g, cols: hid_r[HALF + g : HALF + g + 1, cols],
-        False,
     )
 
     arrived(W_DOWN)
@@ -460,12 +454,9 @@
         0, hid_l,
         lambda g, cols: hid_l[HALF + g : HALF + g + 1, cols],
         lambda g, cols: hid_r[g * 8 : g * 8 + 1, cols],
-        True,
     )
     for i in range(len(rem)):
         sent(i)
-    for t in range(HID // TILE):
-        block_out(t).wait()
 
 
 def on_device(tokens, gain_attn, w_qkv, logit_scale, w_out, gain_ffn, w_up, conv_taps):
@@ -474,8 +465,8 @@
     return pl.pallas_call(
         kernel,
         out_shape=jax.ShapeDtypeStruct((SIDE, SIDE, HID), BF),
-        in_specs=[anywhere] * 3 + [pl.BlockSpec(memory_space=pltpu.SMEM)] + [anywhere] * 4,
-        out_specs=anywhere,
+        in_specs=[anywhere] * 8,
+        out_specs=pl.BlockSpec(memory_space=pltpu.VMEM),
         scratch_shapes=[
             vm((32, SIDE, D), BF),
             vm((KEYS_S, D), BF),
@@ -506,19 +497,20 @@
             vm((HALF + 2 * EDGE, D), BF),
             vm((HALF + EDGE, HID), F32),
             vm((HALF + 2 * EDGE, HID), F32),
-            vm((SIDE, SIDE, HID), BF),
-            pltpu.SemaphoreType.DMA((9,)),
-            pltpu.SemaphoreType.DMA((HID // TILE,)),
+            pltpu.SMEM((HEADS,), F32),
+            pltpu.SemaphoreType.DMA((10,)),
             pltpu.SemaphoreType.DMA((10,)),
             pltpu.SemaphoreType.DMA((10,)),
         ],
         compiler_params=pltpu.CompilerParams(
-            collective_id=0, has_side_effects=True, vmem_limit_bytes=60 * 2**20
+            collective_id=0, has_side_effects=True, vmem_limit_bytes=52 * 2**20
         ),
         name="weather_block",
     )(
-        tokens, gain_attn.reshape(1, D), w_qkv, logit_scale, w_out,
-        gain_ffn.reshape(1, D), w_up, conv_taps,
+        *(pltpu.with_memory_space_constraint(x, pltpu.HBM) for x in (
+            tokens, gain_attn.reshape(1, D), w_qkv, logit_scale, w_out,
+            gain_ffn.reshape(1, D), w_up, conv_taps,
+        ))
     )
 
 

time: 38.7 us -> 35.9 us (0.928)
  Pallas kernels: 36.3 us -> 34.9 us
  local copies, waits for them, and re-layouts: 2.3 us -> 0.97 us
    pallas_call x1, Pallas kernels: 36.3 us -> 34.9 us  [on_device(): pl.pallas_call(kernel, out_shape=jax.ShapeDtypeStruct((SIDE, SIDE, HID),...]
    unnamed x1, local copies, waits for them, and re-layouts: 2.3 us -> 0.97 us
where the time goes in v3:
time: 35.9 us
  Pallas kernels  34.9 us (97%)
  local copies, waits for them, and re-layouts  0.97 us (3%)
    pallas_call x1, Pallas kernels, on_device(): pl.pallas_call(kernel, out_shape=jax.ShapeDtypeStruct((SIDE, SIDE, HID),...  34.9 us
    unnamed x1, local copies, waits for them, and re-layouts  0.97 us

profile of v3, /device:TPU:13, one launch (start us, length us, event | category | flops | bytes accessed | tf_op | source)
XLA Modules:
  0.0 35.9 jit_solution(8599627363327391592)
XLA Ops:
  0.0 34.9 %weather_block.1 = bf16[16,16,2048]{2,1,0:T(8,128)(2,1)S(1)} custom-call(bf16[16,16,1024]{2,1,0:T(8,128)(2,1)} %tok.1, f32[1,1024]{1,0:T(1,128)} %bitcast.2, bf16[1024,1536]{1,0:T(8,128)(2,1)} %wqkv_h.1, f32[8]{0:T(128)} %scale_h.1, bf16[512,1024]{1,0:T(8,128)(2,1)} %wo_h.1, f32[1,1024]{1,0:T(1,128)} %bitcast.3, bf16[1024,2048]{1,0:T(8,128)(2,1)} %wu_h.1, ...), custom_call_target="tpu_custom_call" | custom-call | tf_op jit(solution)/shard_map/weather_block/pallas_call | solution.py:465
  34.9 1.0 %copy.10 = bf16[16,16,2048]{2,1,0:T(8,128)(2,1)} copy(bf16[16,16,2048]{2,1,0:T(8,128)(2,1)S(1)} %weather_block.1) | data formatting | bytes 2097152

commit v4 on v3

--- a/solution.py
+++ b/solution.py
@@ -83,8 +83,7 @@
             (wo_h, wo), (wu_h, wu), (scale_h, scale),
         ))
     ]
-    for c in loc:
-        c.start()
+    loc[L_TOK].start()
 
     def remote(i, src, dst, device):
         return pltpu.make_async_remote_copy(
@@ -110,10 +109,25 @@
         remote(E_DOWN, et.at[low_d], et.at[top_d], below),
         remote(E_UP, et.at[first_d], et.at[bot_d], above),
     ]
+    seam_top, seam_bottom = lat == n_lat // 2 - 1, lat == n_lat // 2
+    seam = seam_top | seam_bottom
+    head = pl.ds(0, CORNER)
+    direct_south = [
+        remote(W_DOWN, send_e.at[low], wt.at[top_d], (lat + 1, east)),
+        remote(E_DOWN, send_w.at[low], et.at[top_d], (lat + 1, west)),
+    ]
+    direct_north = [
+        remote(W_UP, send_e.at[head], wt.at[bot_d], (lat - 1, east)),
+        remote(E_UP, send_w.at[head], et.at[bot_d], (lat - 1, west)),
+    ]
     goes_south, goes_north = (DOWN, W_DOWN, E_DOWN), (UP, W_UP, E_UP)
 
     def start(i):
-        if i in goes_south:
+        if i in (W_DOWN, E_DOWN):
+            pl.when(south_ok & jnp.logical_not(seam_top))(rem[i].start)
+        elif i in (W_UP, E_UP):
+            pl.when(north_ok & jnp.logical_not(seam_bottom))(rem[i].start)
+        elif i in goes_south:
             pl.when(south_ok)(rem[i].start)
         elif i in goes_north:
             pl.when(north_ok)(rem[i].start)
@@ -140,6 +154,13 @@
     for device in (to_e, to_w):
         pl.semaphore_signal(barrier, inc=1, device_id=device, device_id_type=MESH)
 
+    for there, row in ((seam_top, lat + 1), (seam_bottom, lat - 1)):
+
+        @pl.when(there)
+        def _():
+            for device in ((row, east), (row, west)):
+                pl.semaphore_signal(barrier, inc=1, device_id=device, device_id_type=MESH)
+
     @pl.when(south_ok)
     def _():
         pl.semaphore_signal(barrier, inc=1, device_id=below, device_id_type=MESH)
@@ -147,6 +168,56 @@
     @pl.when(north_ok)
     def _():
         pl.semaphore_signal(barrier, inc=1, device_id=above, device_id_type=MESH)
+
+    loc[L_TOK].wait()
+    for c in loc[1:]:
+        c.start()
+    mine = ct[REACH : REACH + SIDE].reshape(SIDE * SIDE, D)
+    slot, source = iota((STRIP, SIDE * SIDE), 0), iota((STRIP, SIDE * SIDE), 1)
+    origin = div7(slot) * (SIDE - REACH) + slot
+
+    def pack(offset):
+        pick = jnp.where(source == origin + offset, 1.0, 0.0).astype(BF)
+        return jnp.dot(pick, mine, preferred_element_type=F32).astype(BF)
+
+    send_e[...] = pack(SIDE - REACH)
+    send_w[...] = pack(0)
+
+    @pl.when(seam)
+    def _():
+        pl.semaphore_wait(barrier, 6)
+
+    @pl.when(south_ok & north_ok & jnp.logical_not(seam))
+    def _():
+        pl.semaphore_wait(barrier, 4)
+
+    @pl.when(jnp.logical_not(south_ok & north_ok))
+    def _():
+        pl.semaphore_wait(barrier, 3)
+
+    start(DOWN)
+    start(UP)
+    late = lon == n_lon - 1
+
+    @pl.when(late)
+    def _():
+        for i in (W_LOW, W_HIGH, E_LOW, E_HIGH):
+            start(i)
+
+    @pl.when(jnp.logical_not(late))
+    def _():
+        for i in (E_LOW, E_HIGH, W_LOW, W_HIGH):
+            start(i)
+
+    def follow(i):
+        pl.when(jnp.logical_not(late))(lambda: start(i))
+
+    for there, copies in ((seam_top, direct_south), (seam_bottom, direct_north)):
+
+        @pl.when(there)
+        def _():
+            for copy in copies:
+                copy.start()
 
     ct[ROWS:, :, :] = jnp.zeros((32 - ROWS, SIDE, D), BF)
     for strip in (wt, et):
@@ -163,43 +234,6 @@
         ct[REACH + SIDE : ROWS, :, :] = jnp.zeros((REACH, SIDE, D), BF)
         for strip in (wt, et):
             strip[CORNER + STRIP : 2 * CORNER + STRIP, :] = jnp.zeros((CORNER, D), BF)
-
-    loc[L_TOK].wait()
-    mine = ct[REACH : REACH + SIDE].reshape(SIDE * SIDE, D)
-    slot, source = iota((STRIP, SIDE * SIDE), 0), iota((STRIP, SIDE * SIDE), 1)
-    origin = div7(slot) * (SIDE - REACH) + slot
-
-    def pack(offset):
-        pick = jnp.where(source == origin + offset, 1.0, 0.0).astype(BF)
-        return jnp.dot(pick, mine, preferred_element_type=F32).astype(BF)
-
-    send_e[...] = pack(SIDE - REACH)
-    send_w[...] = pack(0)
-
-    @pl.when(south_ok & north_ok)
-    def _():
-        pl.semaphore_wait(barrier, 4)
-
-    @pl.when(jnp.logical_not(south_ok & north_ok))
-    def _():
-        pl.semaphore_wait(barrier, 3)
-
-    start(DOWN)
-    start(UP)
-    late = lon == n_lon - 1
-
-    @pl.when(late)
-    def _():
-        for i in (W_LOW, W_HIGH, E_LOW, E_HIGH):
-            start(i)
-
-    @pl.when(jnp.logical_not(late))
-    def _():
-        for i in (E_LOW, E_HIGH, W_LOW, W_HIGH):
-            start(i)
-
-    def follow(i):
-        pl.when(jnp.logical_not(late))(lambda: start(i))
 
     def bias(q_row, q_col, k_row, k_col):
         place = lat * SIDE + k_row
@@ -414,19 +448,17 @@
                     out[r, side * 8 : side * 8 + 8, cols] = gelu(total[r]).astype(BF)
 
     side_middle(et)
+    arrived(W_LOW)
+    start(W_DOWN)
     arrived(E_DOWN)
     arrived(E_UP)
     edge = side_attention(1, et)
-    arrived(W_LOW)
-    start(W_DOWN)
     arrived(W_HIGH)
     start(W_UP)
     loc[L_GF].wait()
     loc[L_TAPS].wait()
     loc[L_WO].wait()
     loc[L_WU].wait()
-    nf[:HALF, :] = ffn_input(attended(slice(HALF, 2 * HALF)), xres[HALF:, :], h >> 3)
-    nf[HALF : HALF + EDGE, :] = ffn_input(attended(edge_rows), edge, e)
     slot, source = iota((EDGE, HALF), 0), iota((EDGE, HALF), 1)
     pick = jnp.where((source == slot * 8 + 7) & (slot < RING), 1.0, 0.0).astype(BF)
     att = jnp.dot(pick, attended(slice(0, HALF)), preferred_element_type=F32).astype(BF)
@@ -434,7 +466,11 @@
     pick = (source == (slot + REACH - 1) * SIDE + 7) & (slot < RING)
     pick = jnp.where(pick, 1.0, 0.0).astype(BF)
     tokens = jnp.dot(pick, ct[...].reshape(KEYS_C, D), preferred_element_type=F32)
-    nf[HALF + EDGE :, :] = ffn_input(att, tokens, e)
+    nf[...] = ffn_input(
+        jnp.concatenate([attended(slice(HALF, 2 * HALF + EDGE)), att], 0),
+        jnp.concatenate([xres[HALF:, :], edge, tokens], 0),
+        jnp.concatenate([h >> 3, e, e], 0),
+    )
 
     up_project(HALF + 2 * EDGE, hid_r)
     side_middle(wt)
@@ -447,8 +483,11 @@
     arrived(W_DOWN)
     arrived(W_UP)
     edge = side_attention(0, wt)
-    nf[:HALF, :] = ffn_input(attended(slice(0, HALF)), xres[:HALF, :], h >> 3)
-    nf[HALF : HALF + EDGE, :] = ffn_input(attended(edge_rows), edge, e)
+    nf[: HALF + EDGE, :] = ffn_input(
+        jnp.concatenate([attended(slice(0, HALF)), attended(edge_rows)], 0),
+        jnp.concatenate([xres[:HALF, :], edge], 0),
+        jnp.concatenate([h >> 3, e], 0),
+    )
     up_project(HALF + EDGE, hid_l)
     filter_half(
         0, hid_l,

time: 35.9 us -> 34.3 us (0.955); the launches traced: 35.9 us -> 33.7 us
  Pallas kernels: 34.9 us -> 32.7 us
    pallas_call x1, Pallas kernels: 34.9 us -> 32.7 us  [on_device(): pl.pallas_call(kernel, out_shape=jax.ShapeDtypeStruct((SIDE, SIDE, HID),...]
where the time goes in v4:
time: 34.3 us; the launch traced here: 33.7 us
  Pallas kernels  32.7 us (95%)
  local copies, waits for them, and re-layouts  0.97 us (3%)
    pallas_call x1, Pallas kernels, on_device(): pl.pallas_call(kernel, out_shape=jax.ShapeDtypeStruct((SIDE, SIDE, HID),...  32.7 us
    unnamed x1, local copies, waits for them, and re-layouts  0.97 us

profile of v4, /device:TPU:13, one launch (start us, length us, event | category | flops | bytes accessed | tf_op | source)
XLA Modules:
  0.0 33.7 jit_solution(2552026921971176796)
XLA Ops:
  0.0 32.7 %weather_block.1 = bf16[16,16,2048]{2,1,0:T(8,128)(2,1)S(1)} custom-call(bf16[16,16,1024]{2,1,0:T(8,128)(2,1)} %tok.1, f32[1,1024]{1,0:T(1,128)} %bitcast.2, bf16[1024,1536]{1,0:T(8,128)(2,1)} %wqkv_h.1, f32[8]{0:T(128)} %scale_h.1, bf16[512,1024]{1,0:T(8,128)(2,1)} %wo_h.1, f32[1,1024]{1,0:T(1,128)} %bitcast.3, bf16[1024,2048]{1,0:T(8,128)(2,1)} %wu_h.1, ...), custom_call_target="tpu_custom_call" | custom-call | tf_op jit(solution)/shard_map/weather_block/pallas_call | solution.py:504
  32.7 1.0 %copy.10 = bf16[16,16,2048]{2,1,0:T(8,128)(2,1)} copy(bf16[16,16,2048]{2,1,0:T(8,128)(2,1)S(1)} %weather_block.1) | data formatting | bytes 2097152

commit v5 on v4

--- a/solution.py
+++ b/solution.py
@@ -32,7 +32,7 @@
 MESH = pl.DeviceIdType.MESH
 FAR = -1e30
 
-DOWN, UP, W_LOW, W_HIGH, E_LOW, E_HIGH, W_DOWN, W_UP, E_DOWN, E_UP = range(10)
+DOWN, UP, W_LOW, W_HIGH, E_LOW, E_HIGH, W_DOWN, W_UP, E_DOWN, E_UP, W_UP2, E_UP2 = range(12)
 L_TOK, L_GA, L_GF, L_TAPS, L_WK, L_WV, L_WQ, L_WO, L_WU, L_SCALE = range(10)
 
 
@@ -95,8 +95,10 @@
     to_e, to_w = (lat, east), (lat, west)
     low, high = pl.ds(CUT, CORNER), pl.ds(0, CUT)
     low_d, high_d = pl.ds(CORNER + CUT, CORNER), pl.ds(CORNER, CUT)
-    top_d, bot_d = pl.ds(0, CORNER), pl.ds(CORNER + STRIP, CORNER)
-    first_d = pl.ds(CORNER, CORNER)
+    top_d = pl.ds(0, CORNER)
+    first_d, second_d = pl.ds(CORNER, CUT), pl.ds(CORNER + CUT, CORNER - CUT)
+    bot_first = pl.ds(CORNER + STRIP, CUT)
+    bot_second = pl.ds(CORNER + STRIP + CUT, CORNER - CUT)
     rem = [
         remote(DOWN, tok.at[pl.ds(SIDE - REACH, REACH)], ct.at[pl.ds(0, REACH)], below),
         remote(UP, tok.at[pl.ds(0, REACH)], ct.at[pl.ds(REACH + SIDE, REACH)], above),
@@ -105,27 +107,31 @@
         remote(E_LOW, send_w.at[low], et.at[low_d], to_w),
         remote(E_HIGH, send_w.at[high], et.at[high_d], to_w),
         remote(W_DOWN, wt.at[low_d], wt.at[top_d], below),
-        remote(W_UP, wt.at[first_d], wt.at[bot_d], above),
+        remote(W_UP, wt.at[first_d], wt.at[bot_first], above),
         remote(E_DOWN, et.at[low_d], et.at[top_d], below),
-        remote(E_UP, et.at[first_d], et.at[bot_d], above),
+        remote(E_UP, et.at[first_d], et.at[bot_first], above),
+        remote(W_UP2, wt.at[second_d], wt.at[bot_second], above),
+        remote(E_UP2, et.at[second_d], et.at[bot_second], above),
     ]
     seam_top, seam_bottom = lat == n_lat // 2 - 1, lat == n_lat // 2
     seam = seam_top | seam_bottom
-    head = pl.ds(0, CORNER)
+    head, neck = pl.ds(0, CUT), pl.ds(CUT, CORNER - CUT)
     direct_south = [
         remote(W_DOWN, send_e.at[low], wt.at[top_d], (lat + 1, east)),
         remote(E_DOWN, send_w.at[low], et.at[top_d], (lat + 1, west)),
     ]
     direct_north = [
-        remote(W_UP, send_e.at[head], wt.at[bot_d], (lat - 1, east)),
-        remote(E_UP, send_w.at[head], et.at[bot_d], (lat - 1, west)),
+        remote(W_UP, send_e.at[head], wt.at[bot_first], (lat - 1, east)),
+        remote(E_UP, send_w.at[head], et.at[bot_first], (lat - 1, west)),
+        remote(W_UP2, send_e.at[neck], wt.at[bot_second], (lat - 1, east)),
+        remote(E_UP2, send_w.at[neck], et.at[bot_second], (lat - 1, west)),
     ]
-    goes_south, goes_north = (DOWN, W_DOWN, E_DOWN), (UP, W_UP, E_UP)
+    goes_south, goes_north = (DOWN, W_DOWN, E_DOWN), (UP, W_UP, E_UP, W_UP2, E_UP2)
 
     def start(i):
         if i in (W_DOWN, E_DOWN):
             pl.when(south_ok & jnp.logical_not(seam_top))(rem[i].start)
-        elif i in (W_UP, E_UP):
+        elif i in (W_UP, E_UP, W_UP2, E_UP2):
             pl.when(north_ok & jnp.logical_not(seam_bottom))(rem[i].start)
         elif i in goes_south:
             pl.when(south_ok)(rem[i].start)
@@ -352,6 +358,7 @@
     keys_values(x, ((0, 0, own), (own, tail, tail_rows)), kc, vc)
     arrived(E_LOW)
     start(E_DOWN)
+    start(E_UP2)
 
     def halves(x):
         x = x.reshape(RING, 2, 8, x.shape[-1])
@@ -450,8 +457,10 @@
     side_middle(et)
     arrived(W_LOW)
     start(W_DOWN)
+    start(W_UP2)
     arrived(E_DOWN)
     arrived(E_UP)
+    arrived(E_UP2)
     edge = side_attention(1, et)
     arrived(W_HIGH)
     start(W_UP)
@@ -482,6 +491,7 @@
 
     arrived(W_DOWN)
     arrived(W_UP)
+    arrived(W_UP2)
     edge = side_attention(0, wt)
     nf[: HALF + EDGE, :] = ffn_input(
         jnp.concatenate([attended(slice(0, HALF)), attended(edge_rows)], 0),
@@ -538,8 +548,8 @@
             vm((HALF + 2 * EDGE, HID), F32),
             pltpu.SMEM((HEADS,), F32),
             pltpu.SemaphoreType.DMA((10,)),
-            pltpu.SemaphoreType.DMA((10,)),
-            pltpu.SemaphoreType.DMA((10,)),
+            pltpu.SemaphoreType.DMA((12,)),
+            pltpu.SemaphoreType.DMA((12,)),
         ],
         compiler_params=pltpu.CompilerParams(
             collective_id=0, has_side_effects=True, vmem_limit_bytes=52 * 2**20

time: 34.3 us -> 34 us (level)
  no operation moved by 1% of the time
where the time goes in v5:
time: 34 us; the launch traced here: 33.4 us
  Pallas kernels  32.4 us (95%)
  local copies, waits for them, and re-layouts  0.97 us (3%)
    pallas_call x1, Pallas kernels, on_device(): pl.pallas_call(kernel, out_shape=jax.ShapeDtypeStruct((SIDE, SIDE, HID),...  32.4 us
    unnamed x1, local copies, waits for them, and re-layouts  0.97 us

profile of v5, /device:TPU:13, one launch (start us, length us, event | category | flops | bytes accessed | tf_op | source)
XLA Modules:
  0.0 33.4 jit_solution(3252559248757401025)
XLA Ops:
  0.0 32.4 %weather_block.1 = bf16[16,16,2048]{2,1,0:T(8,128)(2,1)S(1)} custom-call(bf16[16,16,1024]{2,1,0:T(8,128)(2,1)} %tok.1, f32[1,1024]{1,0:T(1,128)} %bitcast.2, bf16[1024,1536]{1,0:T(8,128)(2,1)} %wqkv_h.1, f32[8]{0:T(128)} %scale_h.1, bf16[512,1024]{1,0:T(8,128)(2,1)} %wo_h.1, f32[1,1024]{1,0:T(1,128)} %bitcast.3, bf16[1024,2048]{1,0:T(8,128)(2,1)} %wu_h.1, ...), custom_call_target="tpu_custom_call" | custom-call | tf_op jit(solution)/shard_map/weather_block/pallas_call | solution.py:514
  32.4 1.0 %copy.10 = bf16[16,16,2048]{2,1,0:T(8,128)(2,1)} copy(bf16[16,16,2048]{2,1,0:T(8,128)(2,1)S(1)} %weather_block.1) | data formatting | bytes 2097152

commit v6 on v5

--- a/solution.py
+++ b/solution.py
@@ -461,9 +461,9 @@
     arrived(E_DOWN)
     arrived(E_UP)
     arrived(E_UP2)
-    edge = side_attention(1, et)
     arrived(W_HIGH)
     start(W_UP)
+    edge = side_attention(1, et)
     loc[L_GF].wait()
     loc[L_TAPS].wait()
     loc[L_WO].wait()

time: 34 us -> 34 us (level)
  no operation moved by 1% of the time
where the time goes in v6:
time: 34 us; the launch traced here: 33.4 us
  Pallas kernels  32.4 us (95%)
  local copies, waits for them, and re-layouts  0.97 us (3%)
    pallas_call x1, Pallas kernels, on_device(): pl.pallas_call(kernel, out_shape=jax.ShapeDtypeStruct((SIDE, SIDE, HID),...  32.4 us
    unnamed x1, local copies, waits for them, and re-layouts  0.97 us

profile of v6, /device:TPU:13, one launch (start us, length us, event | category | flops | bytes accessed | tf_op | source)
XLA Modules:
  0.0 33.4 jit_solution(2369456480851462163)
XLA Ops:
  0.0 32.4 %weather_block.1 = bf16[16,16,2048]{2,1,0:T(8,128)(2,1)S(1)} custom-call(bf16[16,16,1024]{2,1,0:T(8,128)(2,1)} %tok.1, f32[1,1024]{1,0:T(1,128)} %bitcast.2, bf16[1024,1536]{1,0:T(8,128)(2,1)} %wqkv_h.1, f32[8]{0:T(128)} %scale_h.1, bf16[512,1024]{1,0:T(8,128)(2,1)} %wo_h.1, f32[1,1024]{1,0:T(1,128)} %bitcast.3, bf16[1024,2048]{1,0:T(8,128)(2,1)} %wu_h.1, ...), custom_call_target="tpu_custom_call" | custom-call | tf_op jit(solution)/shard_map/weather_block/pallas_call | solution.py:514
  32.4 1.0 %copy.10 = bf16[16,16,2048]{2,1,0:T(8,128)(2,1)} copy(bf16[16,16,2048]{2,1,0:T(8,128)(2,1)S(1)} %weather_block.1) | data formatting | bytes 2097152
